TPU v7x, 32 devices: a whole 2x2x4 slice. The times are simulated.
32 devices in a mesh: child: 2 (over core), row: 4 (over y, x), col: 4 (over z).
Axes of the slice: x: 2, y: 2, z: 4, core: 2. Of those that a mesh axis runs over, the one named last changes fastest.
Arguments:
- schur_blocks: bfloat16 [2, 16384, 16384], P('child', 'row', 'col'), may hold values from -2 to 2
- child_map: int32 [2, 16384], replicated, may hold values from 0 to 24575, as said below
- round_seeds: int32 [2], replicated, may hold values from 1 to 999999
Outputs:
- leaf_bases: float32 [24576, 256], P(('row', 'child', 'col'))
- fresh_samples: float32 [24576, 256], P(('row', 'child', 'col'))
Inputs may be any that keep to these rules, and one draw needn't show every extreme that they name: For each child c and each block r < 4, the entries child_map[c, r * 4096 : (r + 1) * 4096] rise strictly, lie in parent rows [r * 6144, (r + 1) * 6144), and include both ends of that range.
All inputs are finite; a program needn't handle non-finite values.
Results may differ from a plain program's by a relative error of at most 0.0031.
Values sent between devices are 32-bit elements; how exact they have to be, the bound alone decides.
No kernel may reach another device: no remote copies, remote signals or barrier semaphores. Data moves between devices by JAX's collectives and lax.ppermute only.
A program may use at most 128 MiB of HBM per device.

v0:
```python
import jax
import jax.numpy as jnp
from jax import lax
from jax.sharding import PartitionSpec as P

NP = 24576
K = 256


def sample_rows(seed_value, parents, sample_width):
    hashed = (
        parents[:, None] * 40503
        + lax.iota(jnp.int32, sample_width)[None, :] * 9973
        + seed_value * 2654435
    )
    hashed = hashed ^ hashed >> 15 & 131071
    hashed = hashed * 73244475
    hashed = hashed ^ hashed >> 13 & 524287
    hashed = hashed * 1274126177
    hashed = hashed ^ hashed >> 16 & 65535
    unit_value = (hashed & 16777215).astype(jnp.float32) * (1.0 / 16777216.0)
    return (unit_value - 0.5) * 3.4641016


def body(schur_blocks, child_map, round_seeds):
    child_block = schur_blocks[0]
    block_rows, block_cols = child_block.shape
    child_count = lax.axis_size("child")
    col_count = lax.axis_size("col")
    row_count_axis = lax.axis_size("row")
    child_index = lax.axis_index("child")
    row_index = lax.axis_index("row")
    col_index = lax.axis_index("col")
    own_map = lax.dynamic_index_in_dim(child_map, child_index, 0, keepdims=False)
    col_ids = lax.dynamic_slice_in_dim(own_map, col_index * block_cols, block_cols)
    row_ids = lax.dynamic_slice_in_dim(own_map, row_index * block_rows, block_rows)
    leaf_rows = NP // row_count_axis
    own_rows = leaf_rows // (child_count * col_count)
    leaf_base = row_index * leaf_rows

    def sketch_rows(seed_list):
        samples = jnp.concatenate(
            [sample_rows(seed_value, col_ids, K) for seed_value in seed_list], axis=1
        ).astype(jnp.bfloat16)
        return jnp.dot(child_block, samples, preferred_element_type=jnp.float32)

    def extend(partial_value):
        sample_width = partial_value.shape[1]
        window = min(own_rows, block_rows)
        block_total = own_rows * lax.axis_size(("child", "col")) // own_rows
        targets = leaf_base + lax.iota(jnp.int32, block_total) * own_rows
        first_pos = jnp.sum((row_ids[None, :] < targets[:, None]).astype(jnp.int32), axis=1)
        first_pos = jnp.minimum(first_pos, block_rows - window)
        positions = first_pos[:, None] + lax.iota(jnp.int32, window)[None, :]
        parent_ids = jnp.take(row_ids, positions)
        values = jnp.take(partial_value, positions, axis=0)
        wanted = targets[:, None] + lax.iota(jnp.int32, own_rows)[None, :]
        select = (wanted[:, :, None] == parent_ids[:, None, :]).astype(jnp.float32)
        pieces = jnp.einsum("bow,bwk->bok", select, values, precision=lax.Precision.HIGHEST)
        return lax.psum_scatter(
            pieces.reshape(own_rows * lax.axis_size(("child", "col")), sample_width),
            ("child", "col"),
            scatter_dimension=0,
            tiled=True,
        )

    first_leaf = extend(sketch_rows([round_seeds[0]]))
    second_leaf = extend(sketch_rows([round_seeds[1]]))
    gram_local = jnp.dot(first_leaf.T, first_leaf, precision=lax.Precision.HIGHEST)
    gram_matrix = lax.psum(gram_local, ("child", "col")) / leaf_rows
    lower_factor = jnp.linalg.cholesky(gram_matrix)
    leaf_basis = lax.linalg.triangular_solve(
        lower_factor, first_leaf, left_side=False, lower=True, transpose_a=True
    )
    coef_local = jnp.dot(leaf_basis.T, second_leaf, precision=lax.Precision.HIGHEST)
    coefficients = lax.psum(coef_local, ("child", "col")) / leaf_rows
    fresh_samples = second_leaf - jnp.dot(leaf_basis, coefficients, precision=lax.Precision.HIGHEST)
    return (leaf_basis, fresh_samples)


def solution(mesh):
    placed = (P("child", "row", "col"), P(), P())
    return jax.shard_map(
        body,
        mesh=mesh,
        in_specs=placed,
        out_specs=(P(("row", "child", "col"), None), P(("row", "child", "col"), None)),
        check_vma=False,
    )
```

profile of v0, /device:TPU:0, one launch (start us, length us, event | category | flops | bytes accessed | tf_op | source)
XLA Modules:
  0.0 494.6 jit_solution(8860874698210331657)
XLA Ops:
  8.7 1.3 fusion.109
  10.7 17.5 %fusion.18 = f32[4096,256]{0,1:T(8,128)} fusion(bf16[1,4096,4096]{2,1,0:T(8,128)(2,1)} %param.7, s32[]{:T(128)} %bitcast.2, s32[256]{0:T(256)S(1)} %iota_multiply_fusion, s32[4096]{0:T(1024)S(1)} %bitcast.61), kind=kOutput, calls=%fused_computation.25 | convolution fusion | flops 8609857536 | bytes 37766148 | tf_op jit(solution)/shard_map/dot_general | solution.py:45
  28.2 5.6 %copy.15 = f32[4096,256]{1,0:T(8,128)} copy(f32[4096,256]{0,1:T(8,128)} %fusion.18) | data formatting | bytes 8388608 | tf_op jit(solution)/shard_map/dot_general | solution.py:45
  33.9 34.3 %gather_fusion = s32[6144]{0:T(1024)S(1)} fusion(s32[4096]{0:T(1024)S(1)} %bitcast.56, s32[6144]{0:T(1024)S(1)} %broadcast_clamp_fusion), kind=kCustom, calls=%fused_computation.clone | custom fusion | bytes 73728 | tf_op jit(solution)/shard_map/jit(_take)/gather | solution.py:55
  68.1 25.9 %gather_fusion.1 = f32[6144,256]{1,0:T(8,128)} fusion(f32[4096,256]{1,0:T(8,128)} %copy.15, s32[6144]{0:T(1024)S(1)} %broadcast_clamp_fusion), kind=kCustom, calls=%fused_computation.1.clone | custom fusion | bytes 12607488 | tf_op jit(solution)/shard_map/jit(_take)/gather | solution.py:56
  94.2 12.5 %fusion.6 = f32[8,768,256]{2,1,0:T(8,128)} fusion(s32[8,768]{1,0:T(8,128)S(1)} %get-tuple-element.39, s32[8,768]{1,0:T(8,128)S(1)} %get-tuple-element.38, f32[8,768,256]{2,1,0:T(8,128)} %bitcast.60, pred[8,768]{1,0:T(8,128)(4,1)S(1)} %compare_and_fusion), kind=kOutput, calls=%fused_computation.11 | convolution fusion | flops 14501806080 | bytes 12638208 | tf_op jit(solution)/shard_map/bow,bwk->bok/dot_general | solution.py:59
  107.4 18.1 %fusion.21 = f32[4096,256]{0,1:T(8,128)} fusion(bf16[1,4096,4096]{2,1,0:T(8,128)(2,1)} %param.7, s32[]{:T(128)} %bitcast.12, s32[256]{0:T(256)S(1)} %iota_multiply_fusion, s32[4096]{0:T(1024)S(1)} %bitcast.62), kind=kOutput, calls=%fused_computation.26 | convolution fusion | flops 8609857536 | bytes 37766148 | tf_op jit(solution)/shard_map/dot_general | solution.py:45
  125.5 5.6 %copy.18 = f32[4096,256]{1,0:T(8,128)} copy(f32[4096,256]{0,1:T(8,128)} %fusion.21) | data formatting | bytes 8388608 | tf_op jit(solution)/shard_map/dot_general | solution.py:45
  131.2 26.0 %gather_fusion.2 = f32[6144,256]{1,0:T(8,128)} fusion(f32[4096,256]{1,0:T(8,128)} %copy.18, s32[6144]{0:T(1024)S(1)} %broadcast_clamp_fusion), kind=kCustom, calls=%fused_computation.2.clone | custom fusion | bytes 12607488 | tf_op jit(solution)/shard_map/jit(_take)/gather | solution.py:56
  157.1 80.3 %reduce-scatter.3.cloned.1.call-done = f32[768,256]{1,0:T(8,128)} async-done(((f32[6144,256]{1,0:T(8,128)}), f32[768,256]{1,0:T(8,128)}) %reduce-scatter.3.cloned.1.call-update) | async-done | bytes 786448 | tf_op jit(solution)/shard_map/reduce_scatter | solution.py:60
  237.4 3.6 fusion.110
  241.3 12.5 %fusion.4 = f32[8,768,256]{2,1,0:T(8,128)} fusion(s32[8,768]{1,0:T(8,128)S(1)} %get-tuple-element.39, s32[8,768]{1,0:T(8,128)S(1)} %get-tuple-element.38, f32[8,768,256]{2,1,0:T(8,128)} %bitcast.59, pred[8,768]{1,0:T(8,128)(4,1)S(1)} %compare_and_fusion), kind=kOutput, calls=%fused_computation.9 | convolution fusion | flops 14501806080 | bytes 12638208 | tf_op jit(solution)/shard_map/bow,bwk->bok/dot_general | solution.py:59
  253.9 42.7 %all-reduce.4.cloned.1.call-done = f32[256,256]{0,1:T(8,128)} async-done(((f32[256,256]{0,1:T(8,128)}), f32[256,256]{0,1:T(8,128)}) %all-reduce.4.cloned.1.call-update) | async-done | bytes 262160 | tf_op jit(solution)/shard_map/psum | solution.py:70
  298.8 11.7 %cholesky.50 = f32[128,128]{1,0:T(8,128)S(1)} custom-call(f32[128,128]{1,0:T(8,128)S(1)} %cholesky.118), custom_call_target="Cholesky" | custom-call | tf_op jit(solution)/shard_map/jit(cholesky)/cholesky | solution.py:71
  310.6 9.8 %custom-call.14 = f32[1,128,128]{1,2,0:T(8,128)S(1)} custom-call(f32[1,128,128]{2,1,0:T(8,128)S(1)} %get-tuple-element.33), custom_call_target="InvertDiagBlocksLowerTriangular" | custom-call | tf_op jit(solution)/shard_map/jit(cholesky)/cholesky | solution.py:71
  320.9 11.7 %cholesky.105 = f32[128,128]{1,0:T(8,128)S(1)} custom-call(f32[128,128]{1,0:T(8,128)S(1)} %convolution_subtract_fusion.2), custom_call_target="Cholesky" | custom-call | tf_op jit(solution)/shard_map/jit(cholesky)/cholesky | solution.py:71
  335.3 4.1 while.1
  336.1 1.4 bitcast_dynamic-update-slice_fusion.2
  338.1 1.4 bitcast_dynamic-update-slice_fusion.2
  339.5 19.7 %custom-call.15 = f32[2,128,128]{1,2,0:T(8,128)S(1)} custom-call(f32[2,128,128]{2,1,0:T(8,128)S(1)} %get-tuple-element.11), custom_call_target="InvertDiagBlocksLowerTriangular" | custom-call | tf_op jit(solution)/shard_map/triangular_solve | solution.py:72
  361.0 65.0 %reduce-scatter.5.cloned.1.call-done = f32[768,256]{1,0:T(8,128)} async-done(((f32[6144,256]{1,0:T(8,128)}), f32[768,256]{1,0:T(8,128)}) %reduce-scatter.5.cloned.1.call-update) | async-done | bytes 786448 | tf_op jit(solution)/shard_map/reduce_scatter | solution.py:60
  426.0 3.3 fusion.107
  430.6 54.3 %all-reduce.6.cloned.1.call-done = f32[256,256]{0,1:T(8,128)} async-done(((f32[256,256]{0,1:T(8,128)}), f32[256,256]{0,1:T(8,128)}) %all-reduce.6.cloned.1.call-update) | async-done | bytes 262160 | tf_op jit(solution)/shard_map/psum | solution.py:76
  484.9 3.2 convolution_subtract_fusion
  (47 shorter events, 10.2 us)
Async XLA Ops:
  7.2 230.3 %reduce-scatter.3.cloned.1.call-start = ((), (), s32[]{:S(2)}) async-start(), calls=%async_computation.2 | async-start | bytes 7077888 | tf_op jit(solution)/shard_map/reduce_scatter | solution.py:60
  106.7 190.0 %all-reduce.4.cloned.1.call-start = ((), (), s32[]{:S(2)}) async-start(), calls=%async_computation.3 | async-start | bytes 524288 | tf_op jit(solution)/shard_map/psum | solution.py:70
  241.1 184.9 %reduce-scatter.5.cloned.1.call-start = ((), (), s32[]{:S(2)}) async-start(), calls=%async_computation.4 | async-start | bytes 7077888 | tf_op jit(solution)/shard_map/reduce_scatter | solution.py:60
  253.8 105.3 %copy-start = (f32[768,256]{1,0:T(8,128)S(1)}, f32[768,256]{1,0:T(8,128)}, u32[]{:S(2)}) copy-start(f32[768,256]{1,0:T(8,128)} %reduce-scatter.3.cloned.1.call-done) | copy-start | bytes 2359300
  253.9 231.0 %all-reduce.6.cloned.1.call-start = ((), (), s32[]{:S(2)}) async-start(), calls=%async_computation.5 | async-start | bytes 524288 | tf_op jit(solution)/shard_map/psum | solution.py:76
  426.0 58.8 %copy-start.1 = (f32[768,256]{1,0:T(8,128)S(1)}, f32[768,256]{1,0:T(8,128)}, u32[]{:S(2)}) copy-start(f32[768,256]{1,0:T(8,128)} %reduce-scatter.5.cloned.1.call-done) | copy-start | bytes 2359300
Sparse Core Ops, SparseCore 0:
  106.8 130.5 reduce-scatter.2
  241.2 55.4 all-reduce.3
  299.1 126.8 reduce-scatter.4
  429.5 55.3 all-reduce.5
where the time goes:
time: 495 us
  waiting for transfers between devices  242 us (49%)
  local copies, waits for them, and re-layouts  104 us (21%)
  matrix products  73.2 us (15%)
  other arithmetic  57.8 us (12%)
  between operations  16.6 us (3%)
    reduce_scatter x2, waiting for transfers between devices, extend(): lax.psum_scatter(pieces.reshape(own_rows * lax.axis_size(('child', 'col')...  145 us
    psum x1, waiting for transfers between devices, body(): coefficients = lax.psum(coef_local, ('child', 'col')) / leaf_rows  54.3 us
    gather x2, local copies, waits for them, and re-layouts, extend(): values = jnp.take(partial_value, positions, axis=0)  51.9 us
    psum x1, waiting for transfers between devices, body(): gram_matrix = lax.psum(gram_local, ('child', 'col')) / leaf_rows  42.7 us
    dot_general x2, matrix products, sketch_rows(): return jnp.dot(child_block, samples, preferred_element_type=jnp.float32)  35.7 us
    another operation x7, other arithmetic, body(): lower_factor = jnp.linalg.cholesky(gram_matrix)  34.6 us
    gather x2, local copies, waits for them, and re-layouts, extend(): parent_ids = jnp.take(row_ids, positions)  34.3 us
    dot_general x2, matrix products, extend(): jnp.einsum('bow,bwk->bok', select, values, precision=lax.Precision.HIGHEST)  25 us
  transfers between devices with their start and end apart: 4, of which 4 were waited for; matrix products, arithmetic and copies ran while one was open for 26% of the time, Pallas kernels for 0%

commit v1 on v0

v1 whole, which is shorter than its diff:
```python
import functools

import jax
import jax.numpy as jnp
import numpy as np
from jax import lax
from jax.experimental import pallas as pl
from jax.experimental.pallas import tpu as pltpu
from jax.sharding import PartitionSpec as P

NP = 24576
K = 256
HI = lax.Precision.HIGHEST
CORES = [(0, 1), (1, 0)]
MIB = 1024 * 1024


def sample_rows(seed_value, parents, sample_width):
    hashed = (
        parents[:, None] * 40503
        + lax.iota(jnp.int32, sample_width)[None, :] * 9973
        + seed_value * 2654435
    )
    hashed = hashed ^ hashed >> 15 & 131071
    hashed = hashed * 73244475
    hashed = hashed ^ hashed >> 13 & 524287
    hashed = hashed * 1274126177
    hashed = hashed ^ hashed >> 16 & 65535
    unit_value = (hashed & 16777215).astype(jnp.float32) * (1.0 / 16777216.0)
    return (unit_value - 0.5) * 3.4641016


def block_sizes(own_rows, block_rows):
    piece = own_rows // 2 if own_rows % 32 == 0 and own_rows >= 256 else own_rows
    window = min(piece + 16, block_rows)
    tile = max(d for d in range(8, min(piece, 240) + 1, 8) if piece % d == 0)
    reach = min(256, window)
    return piece, window, tile, reach


def block_kernel(sizes, steps, scal_ref, ids_ref, schur_ref, samples_ref, *rest):
    piece, window, tile, reach = sizes
    mine_ref, other_ref, held, total, sems = rest[-5:]
    depth = held.shape[0]
    step = pl.program_id(0)

    def copy(s):
        slot = lax.rem(s, depth)
        first = pl.multiple_of(scal_ref[s, 0], 16)
        return pltpu.make_async_copy(schur_ref.at[pl.ds(first, window), :], held.at[slot], sems.at[slot])

    @pl.when(step == 0)
    def _():
        for s in range(min(depth - 1, steps)):
            copy(s).start()

    @pl.when(step + depth - 1 < steps)
    def _():
        copy(step + depth - 1).start()

    copy(step).wait()
    total[...] = jnp.dot(
        held[lax.rem(step, depth)], samples_ref[...], preferred_element_type=jnp.float32
    )

    def spread(out_ref):
        for i in range(piece // tile):
            first = pl.multiple_of(scal_ref[step, 2 + i], 16)
            child = scal_ref[step, 0] + first
            lane = pl.multiple_of(child // 128 * 128, 128)
            ids = pltpu.roll(ids_ref[:, pl.ds(lane, 384)], lax.rem(384 - (child - lane), 384), 1)
            ids = jnp.broadcast_to(ids[0:1, :reach], (tile, reach))
            wanted = scal_ref[step, 1] + i * tile + lax.broadcasted_iota(jnp.int32, (tile, reach), 0)
            select = (ids == wanted).astype(jnp.float32).astype(jnp.bfloat16)
            values = total[pl.ds(first, reach), :]
            high = values.astype(jnp.bfloat16)
            low = (values - high.astype(jnp.float32)).astype(jnp.bfloat16)
            out_ref[i * tile : (i + 1) * tile, :] = jnp.dot(
                select, high, preferred_element_type=jnp.float32
            ) + jnp.dot(select, low, preferred_element_type=jnp.float32)

    @pl.when(lax.rem(step, 2) == 0)
    def _():
        spread(other_ref)

    @pl.when(lax.rem(step, 2) == 1)
    def _():
        spread(mine_ref)


def block_scalars(row_ids, bases, own_rows, sizes):
    piece, window, tile, reach = sizes
    block_rows = row_ids.shape[0]
    bases = (bases.reshape(-1, 1, 2)[:, :, ::-1] + lax.iota(jnp.int32, own_rows // piece)[None, :, None] * piece).reshape(-1)
    starts = bases[:, None] + lax.iota(jnp.int32, piece // tile)[None, :] * tile
    before = jnp.sum((row_ids[None, None, :] < starts[:, :, None]).astype(jnp.int32), axis=2)
    first = jnp.minimum(before[:, :1] // 16 * 16, block_rows - window)
    inner = jnp.minimum((before - first) // 16 * 16, window - reach)
    return jnp.concatenate([first, bases[:, None], inner], axis=1)


def sketch_pair(scalars, ids, child_block, samples, own_rows, sizes, after=()):
    piece, window, _, _ = sizes
    steps = scalars.shape[0]
    block_cols = child_block.shape[1]
    width = samples.shape[1]
    grid_spec = pltpu.PrefetchScalarGridSpec(
        num_scalar_prefetch=1,
        grid=(steps,),
        in_specs=[
            pl.BlockSpec(memory_space=pltpu.VMEM),
            pl.BlockSpec(memory_space=pl.ANY),
            pl.BlockSpec(memory_space=pltpu.VMEM),
        ]
        + [pl.BlockSpec(memory_space=pl.ANY)] * len(after),
        out_specs=[pl.BlockSpec((piece, width), lambda s, _: (s // 2, 0))] * 2,
        scratch_shapes=[
            pltpu.VMEM((3, window, block_cols), jnp.bfloat16),
            pltpu.VMEM((window, width), jnp.float32),
            pltpu.SemaphoreType.DMA((3,)),
        ],
    )
    return pl.pallas_call(
        functools.partial(block_kernel, sizes, steps),
        out_shape=[jax.ShapeDtypeStruct((own_rows, width), jnp.float32)] * 2,
        grid_spec=grid_spec,
        compiler_params=pltpu.CompilerParams(vmem_limit_bytes=24 * MIB),
        cost_estimate=pl.CostEstimate(
            flops=2 * steps * window * block_cols * width,
            bytes_accessed=2 * steps * window * block_cols,
            transcendentals=0,
        ),
        name="sketch",
    )(scalars, ids, child_block, samples, *after)


def eliminate(tiles, size):
    count = size // 8
    sub = lax.broadcasted_iota(jnp.int32, (8, size), 0)
    lane = lax.broadcasted_iota(jnp.int32, (8, size), 1)
    rows = list(tiles)
    inverse = [(lane == sub + 8 * t).astype(jnp.float32) for t in range(count)]

    def row(value, k):
        return jnp.broadcast_to(value[k : k + 1, :], (8, size))

    for t in range(count):
        columns = [
            [jnp.broadcast_to(rows[i][:, 8 * t + k : 8 * t + k + 1], (8, size)) for k in range(8)]
            for i in range(t, count)
        ]
        diagonal = jnp.ones((8, size), jnp.float32)
        for k in range(8):
            pivot = row(columns[0][k], k)
            scale = 1.0 / pivot
            diagonal = jnp.where(sub == k, pivot, diagonal)
            heads = [row(columns[0][l], k) * scale for l in range(k + 1, 8)]
            head_row = row(rows[t], k) * scale
            head_inv = row(inverse[t], k) * scale
            for i in range(t, count):
                factor = columns[i - t][k]
                if i == t:
                    factor = jnp.where(sub > k, factor, 0.0)
                for l in range(k + 1, 8):
                    columns[i - t][l] = columns[i - t][l] - factor * heads[l - k - 1]
                rows[i] = rows[i] - factor * head_row
                inverse[i] = inverse[i] - factor * head_inv
        inverse[t] = inverse[t] * lax.rsqrt(diagonal)
    return jnp.concatenate(inverse, axis=0)


def factor_kernel(gram_ref, out_ref):
    half = gram_ref.shape[0] // 2

    def dot(a, b, dims):
        return lax.dot_general(a, b, (dims, ((), ())), precision=HI, preferred_element_type=jnp.float32)

    first = eliminate([gram_ref[8 * t : 8 * t + 8, :half] for t in range(half // 8)], half)
    lower = dot(gram_ref[half:, :half], first, ((1,), (1,)))
    rest = gram_ref[half:, half:] - dot(lower, lower, ((1,), (1,)))
    second = eliminate([rest[8 * t : 8 * t + 8, :] for t in range(half // 8)], half)
    out_ref[:half, :half] = first
    out_ref[:half, half:] = jnp.zeros((half, half), jnp.float32)
    out_ref[half:, :half] = -dot(second, dot(lower, first, ((1,), (0,))), ((1,), (0,)))
    out_ref[half:, half:] = second


def inverse_factor(gram):
    return pl.pallas_call(
        factor_kernel,
        out_shape=jax.ShapeDtypeStruct(gram.shape, jnp.float32),
        compiler_params=pltpu.CompilerParams(vmem_limit_bytes=16 * MIB),
        name="inverse_factor",
    )(gram)


ORDER = np.array([[3, 2, 1, 0], [3, 2, 0, 1], [0, 1, 3, 2], [0, 1, 2, 3]], np.int32)
INWARD = [(0, 1), (3, 2)]
ACROSS = [(1, 2), (2, 1)]
PAIRS = [(0, 1), (1, 0), (2, 3), (3, 2)]


def hop(value, pairs):
    return lax.ppermute(value, "col", pairs)


def line_scatter(make, after):
    own0 = make(0, after[0])
    in3 = [hop(own, INWARD) for own in own0]
    own1 = make(1, after[1] if 1 in after else own0[:1])
    mid1 = [hop(own + step, ACROSS) for own, step in zip(own0, in3)]
    in2 = [hop(own, INWARD) for own in own1]
    own2 = make(2, mid1[:1])
    mid2 = [hop(own + step, ACROSS) for own, step in zip(own1, in2)]
    own3 = make(3, mid1[1:])
    last = [hop(own + step, PAIRS) for own, step in zip(own2, mid1)]
    return [sum(terms) for terms in zip(own3, mid2, last)], [mid2[0], last[0]]


def line_sum(value):
    value = value + hop(value, PAIRS)
    return value + hop(value, [(0, 2), (2, 0), (1, 3), (3, 1)])


def group_sum(value, child_index):
    half = value.shape[0] // 2
    mine = lax.dynamic_slice_in_dim(value, child_index * half, half)
    other = lax.dynamic_slice_in_dim(value, (1 - child_index) * half, half)
    mine = line_sum(mine + lax.ppermute(other, "child", CORES))
    other = lax.ppermute(mine, "child", CORES)
    low = jnp.where(child_index == 0, mine, other)
    high = jnp.where(child_index == 0, other, mine)
    return jnp.concatenate([low, high], axis=0)


def body(schur_blocks, child_map, round_seeds):
    child_block = schur_blocks[0]
    block_rows, block_cols = child_block.shape
    child_count = lax.axis_size("child")
    col_count = lax.axis_size("col")
    row_count = lax.axis_size("row")
    child_index = lax.axis_index("child")
    row_index = lax.axis_index("row")
    col_index = lax.axis_index("col")
    own_map = lax.dynamic_index_in_dim(child_map, child_index, 0, keepdims=False)
    col_ids = lax.dynamic_slice_in_dim(own_map, col_index * block_cols, block_cols)
    row_ids = lax.dynamic_slice_in_dim(own_map, row_index * block_rows, block_rows)
    leaf_rows = NP // row_count
    own_rows = leaf_rows // (child_count * col_count)
    leaf_base = row_index * leaf_rows
    sizes = block_sizes(own_rows, block_rows)
    ids = jnp.broadcast_to(jnp.pad(row_ids, (0, 384), constant_values=-1)[None, :], (8, block_rows + 384))
    samples = [
        sample_rows(round_seeds[r], col_ids, K).astype(jnp.bfloat16) for r in range(round_seeds.shape[0])
    ]

    if child_count == 2 and col_count == len(ORDER):
        places = lax.dynamic_index_in_dim(jnp.asarray(ORDER), col_index, 0, keepdims=False)
        halves = jnp.stack([child_index, 1 - child_index])
        bases = leaf_base + (halves[None, :] * col_count + places[:, None]) * own_rows
        scalars = block_scalars(row_ids, bases.reshape(-1), own_rows, sizes)

        pieces = 2 * (own_rows // sizes[0])

        def maker(r):
            def make(p, after):
                mine, other = sketch_pair(
                    scalars[pieces * p : pieces * (p + 1)], ids, child_block, samples[r], own_rows, sizes, after
                )
                other = lax.ppermute(other, "child", CORES)
                own = [mine[:, c : c + K // 2] + other[:, c : c + K // 2] for c in (0, K // 2)]
                return lax.optimization_barrier(own)

            return make

        def total(value):
            return group_sum(value, child_index)

        first_parts, steps = line_scatter(maker(0), {0: []})
        first_leaf = jnp.concatenate(first_parts, axis=1)
        second_parts, _ = line_scatter(maker(1), {0: steps[:1], 1: steps[1:]})
    else:
        places = lax.iota(jnp.int32, child_count * col_count)
        scalars = block_scalars(row_ids, leaf_base + places * own_rows, own_rows, sizes)

        pieces = own_rows // sizes[0]

        def leaf(r):
            blocks = []
            for p in range(0, child_count * col_count, 2):
                blocks += sketch_pair(scalars[p * pieces : (p + 2) * pieces], ids, child_block, samples[r], own_rows, sizes)
            return lax.psum_scatter(
                jnp.concatenate(blocks, axis=0), ("child", "col"), scatter_dimension=0, tiled=True
            )

        def total(value):
            return lax.psum(value, ("child", "col"))

        first_leaf = leaf(0)
        second_parts = [leaf(1)]

    gram = total(jnp.dot(first_leaf.T, first_leaf, precision=HI)) / leaf_rows
    inverse = inverse_factor(gram)
    leaf_basis = lax.dot_general(first_leaf, inverse, (((1,), (1,)), ((), ())), precision=HI)
    dual = jnp.dot(leaf_basis, inverse, precision=HI)
    fresh = []
    for second in second_parts:
        cross = total(jnp.dot(first_leaf.T, second, precision=HI)) / leaf_rows
        fresh.append(second - jnp.dot(dual, cross, precision=HI))
    return (leaf_basis, jnp.concatenate(fresh, axis=1))


def solution(mesh):
    placed = (P("child", "row", "col"), P(), P())
    return jax.shard_map(
        body,
        mesh=mesh,
        in_specs=placed,
        out_specs=(P(("row", "child", "col"), None), P(("row", "child", "col"), None)),
        check_vma=False,
    )
```

time: 495 us -> 237 us (0.48)
  waiting for transfers between devices: 242 us -> 61.3 us
  local copies, waits for them, and re-layouts: 104 us -> 8.65 us
  Pallas kernels: 0 us -> 78.2 us
  matrix products: 73.2 us -> 7.51 us
  starting transfers between devices: 0.34 us -> 55.8 us
  other arithmetic: 57.8 us -> 21.6 us
  between operations: 16.6 us -> 2.77 us
    reduce_scatter x2 -> x0, waiting for transfers between devices: 145 us -> none  [extend(): lax.psum_scatter(pieces.reshape(own_rows * lax.axis_size(('child', 'col')...]
    psum x2 -> x0, waiting for transfers between devices: 97 us -> none  [the longest x1 54.3 us: body(): coefficients = lax.psum(coef_local, ('child', 'col')) / leaf_rows]
    gather x4 -> x0, local copies, waits for them, and re-layouts: 86.2 us -> none  [the longest x2 51.9 us: extend(): values = jnp.take(partial_value, positions, axis=0)]
    pallas_call x0 -> x9, Pallas kernels: none -> 78.2 us  [the longest x8 69.2 us: sketch_pair(): pl.pallas_call(functools.partial(block_kernel, sizes, steps), out_shape=[...]
    dot_general x7, matrix products: 70.9 us -> 7.51 us  [the longest x2 2.85 us: body(): cross = total(jnp.dot(first_leaf.T, second, precision=HI)) / leaf_rows]
    ppermute x0 -> x40, waiting for transfers between devices: none -> 61.3 us  [the longest x26 57.9 us: hop(): return lax.ppermute(value, 'col', pairs)]
    ppermute x0 -> x40, starting transfers between devices: none -> 55.8 us  [the longest x26 53.2 us: hop(): return lax.ppermute(value, 'col', pairs)]
    another operation x11 -> x1, other arithmetic: 54.4 us -> 0.01 us  [the longest x7 34.6 us: body(): lower_factor = jnp.linalg.cholesky(gram_matrix)]
  transfers between devices with their start and end apart: 4 -> 40, of which waited for: 4 -> 12; matrix products, arithmetic and copies ran while one was open for 26% -> 8% of each run, Pallas kernels for 0% -> 26%
where the time goes in v1:
time: 237 us; the launch traced here: 236 us
  Pallas kernels  78.2 us (33%)
  waiting for transfers between devices  61.3 us (26%)
  starting transfers between devices  55.8 us (24%)
  other arithmetic  21.6 us (9%)
  local copies, waits for them, and re-layouts  8.65 us (4%)
  matrix products  7.51 us (3%)
  between operations  2.77 us (1%)
    pallas_call x8, Pallas kernels, sketch_pair(): pl.pallas_call(functools.partial(block_kernel, sizes, steps), out_shape=[...  69.2 us
    ppermute x26, waiting for transfers between devices, hop(): return lax.ppermute(value, 'col', pairs)  57.9 us
    ppermute x26, starting transfers between devices, hop(): return lax.ppermute(value, 'col', pairs)  53.2 us
    pallas_call x1, Pallas kernels, inverse_factor(): pl.pallas_call(factor_kernel, out_shape=jax.ShapeDtypeStruct(gram.shape,...  8.93 us
    add x8, other arithmetic, make(): own = [mine[:, c:c + K // 2] + other[:, c:c + K // 2] for c in (0, K // 2)]  8.35 us
    unnamed x34, local copies, waits for them, and re-layouts  6.24 us
    convert_element_type x1, other arithmetic, body(): sample_rows(round_seeds[r], col_ids, K).astype(jnp.bfloat16)  4.99 us
  transfers between devices with their start and end apart: 40, of which 12 were waited for; matrix products, arithmetic and copies ran while one was open for 8% of the time, Pallas kernels for 26%

profile of v1, /device:TPU:0, one launch (start us, length us, event | category | flops | bytes accessed | tf_op | source)
XLA Modules:
  0.0 235.7 jit_solution(90100251073093354)
XLA Ops:
  6.0 5.0 %multiply_convert_fusion = (bf16[4096,256]{1,0:T(8,128)(2,1)S(1)}, bf16[4096,256]{1,0:T(8,128)(2,1)S(1)}) fusion(s32[]{:T(128)} %bitcast.8, s32[256]{0:T(256)S(1)} %iota_multiply_fusion, s32[4096]{0:T(1024)S(1)} %bitcast.26, s32[]{:T(128)} %bitcast.7), kind=kLoop, calls=%fused_computation.18 | loop fusion | flops 38797312 | bytes 4211720 | tf_op jit(solution)/shard_map/convert_element_type | solution.py:254
  11.0 8.9 %sketch.8 = (f32[768,256]{1,0:T(8,128)S(1)}, f32[768,256]{1,0:T(8,128)}) custom-call(s32[4,4]{1,0:T(4,128)S(1)} %copy.27.scal_ref, s32[8,4480]{1,0:T(8,128)S(1)} %broadcast_in_dim.2.ids_ref, bf16[4096,4096]{1,0:T(8,128)(2,1)} %bitcast.16, bf16[4096,256]{1,0:T(8,128)(2,1)S(1)} %get-tuple-element.91.samples_ref), custom_call_target="tpu_custom_call" | custom-call | flops 3355443200 | bytes 13107200 | tf_op jit(solution)/shard_map/sketch/pallas_call | solution.py:123
  25.6 8.0 %sketch.10 = (f32[768,256]{1,0:T(8,128)S(1)}, f32[768,256]{1,0:T(8,128)S(1)}) custom-call(s32[4,4]{1,0:T(4,128)S(1)} %copy.28.scal_ref, s32[8,4480]{1,0:T(8,128)S(1)} %broadcast_in_dim.2.ids_ref, bf16[4096,4096]{1,0:T(8,128)(2,1)} %bitcast.17, bf16[4096,256]{1,0:T(8,128)(2,1)S(1)} %copy-done.1, f32[768,128]{1,0:T(8,128)S(1)} %get-tuple-element.40.rest_0_), custom_call_target="tpu_custom_call" | custom-call | flops 3355443200 | bytes 13107200 | tf_op jit(solution)/shard_map/sketch/pallas_call | solution.py:123
  34.0 4.6 %collective-permute-start.7 = (f32[768,128]{1,0:T(8,128)S(1)}, f32[768,128]{1,0:T(8,128)S(1)}, u32[]{:S(2)}, u32[]{:S(2)}) collective-permute-start(f32[768,128]{1,0:T(8,128)S(1)} %get-tuple-element.40.rest_0_), channel_id=1, source_target_pairs={{0,1},{3,2},{4,5},{7,6},{8,9},{11,10},{12,13},{15,14},{16,17},{19,... | collective-permute-start | bytes 1179656 | tf_op jit(solution)/shard_map/ppermute | solution.py:204
  42.9 5.2 %collective-permute-done.7 = f32[768,128]{1,0:T(8,128)S(1)} collective-permute-done((f32[768,128]{1,0:T(8,128)S(1)}, f32[768,128]{1,0:T(8,128)S(1)}, u32[]{:S(2)}, u32[]{:S(2)}) %collective-permute-start.7) | collective-permute-done | bytes 393248 | tf_op jit(solution)/shard_map/ppermute | solution.py:204
  49.5 7.0 %collective-permute-done.1 = f32[768,128]{1,0:T(8,128)S(1)} collective-permute-done((f32[768,128]{1,0:T(8,128)S(1)}, f32[768,128]{1,0:T(8,128)S(1)}, u32[]{:S(2)}, u32[]{:S(2)}) %collective-permute-start.1) | collective-permute-done | bytes 393248 | tf_op jit(solution)/shard_map/ppermute | solution.py:204
  58.2 6.2 %collective-permute-done.5 = f32[768,128]{1,0:T(8,128)} collective-permute-done((f32[768,128]{1,0:T(8,128)S(1)}, f32[768,128]{1,0:T(8,128)}, u32[]{:S(2)}, u32[]{:S(2)}) %collective-permute-start.5) | collective-permute-done | bytes 393248 | tf_op jit(solution)/shard_map/ppermute | solution.py:204
  67.7 8.9 %sketch.11 = (f32[768,256]{1,0:T(8,128)S(1)}, f32[768,256]{1,0:T(8,128)}) custom-call(s32[4,4]{1,0:T(4,128)S(1)} %copy.29.scal_ref, s32[8,4480]{1,0:T(8,128)S(1)} %broadcast_in_dim.2.ids_ref, bf16[4096,4096]{1,0:T(8,128)(2,1)} %bitcast.18, bf16[4096,256]{1,0:T(8,128)(2,1)S(1)} %copy-done.2, f32[768,128]{1,0:T(8,128)S(1)} %collective-permute-done.8.rest_0_), custom_call_target="tpu_custom_call" | custom-call | flops 3355443200 | bytes 13107200 | tf_op jit(solution)/shard_map/sketch/pallas_call | solution.py:123
  77.5 8.9 %sketch.9 = (f32[768,256]{1,0:T(8,128)S(1)}, f32[768,256]{1,0:T(8,128)}) custom-call(s32[4,4]{1,0:T(4,128)S(1)} %copy.26.scal_ref, s32[8,4480]{1,0:T(8,128)S(1)} %broadcast_in_dim.2.ids_ref, bf16[4096,4096]{1,0:T(8,128)(2,1)} %bitcast.19, bf16[4096,256]{1,0:T(8,128)(2,1)S(1)} %copy-done.2, f32[768,128]{1,0:T(8,128)S(1)} %collective-permute-done.2.rest_0_), custom_call_target="tpu_custom_call" | custom-call | flops 3355443200 | bytes 13107200 | tf_op jit(solution)/shard_map/sketch/pallas_call | solution.py:123
  86.9 8.0 %collective-permute-start.11 = (f32[768,128]{1,0:T(8,128)}, f32[768,128]{1,0:T(8,128)}, u32[]{:S(2)}, u32[]{:S(2)}) collective-permute-start(f32[768,128]{1,0:T(8,128)} %get-tuple-element.48), channel_id=1, source_target_pairs={{0,1},{3,2},{4,5},{7,6},{8,9},{11,10},{12,13},{15,14},{16,17},{19,... | collective-permute-start | bytes 1179656 | tf_op jit(solution)/shard_map/ppermute | solution.py:204
  94.9 8.9 %sketch.12 = (f32[768,256]{1,0:T(8,128)S(1)}, f32[768,256]{1,0:T(8,128)}) custom-call(s32[4,4]{1,0:T(4,128)S(1)} %copy.27.scal_ref, s32[8,4480]{1,0:T(8,128)S(1)} %broadcast_in_dim.2.ids_ref, bf16[4096,4096]{1,0:T(8,128)(2,1)} %bitcast.20, bf16[4096,256]{1,0:T(8,128)(2,1)S(1)} %get-tuple-element.90.samples_ref, f32[768,128]{1,0:T(8,128)S(1)} %collective-permute-done.6.rest_0_), custom_call_target="tpu_custom_call" | custom-call | flops 3355443200 | bytes 13107200 | tf_op jit(solution)/shard_map/sketch/pallas_call | solution.py:123
  113.2 3.9 %collective-permute-start.25 = (f32[768,128]{1,0:T(8,128)S(1)}, f32[768,128]{1,0:T(8,128)S(1)}, u32[]{:S(2)}, u32[]{:S(2)}) collective-permute-start(f32[768,128]{1,0:T(8,128)S(1)} %get-tuple-element.59), channel_id=1, source_target_pairs={{0,1},{3,2},{4,5},{7,6},{8,9},{11,10},{12,13},{15,14},{16,17},{19,... | collective-permute-start | bytes 1179656 | tf_op jit(solution)/shard_map/ppermute | solution.py:204
  117.1 11.5 %collective-permute-done.10.rest_0_ = f32[768,128]{1,0:T(8,128)S(1)} collective-permute-done((f32[768,128]{1,0:T(8,128)S(1)}, f32[768,128]{1,0:T(8,128)S(1)}, u32[]{:S(2)}, u32[]{:S(2)}) %collective-permute-start.10) | collective-permute-done | bytes 393248 | tf_op jit(solution)/shard_map/ppermute | solution.py:204
  128.6 8.0 %sketch.14 = (f32[768,256]{1,0:T(8,128)S(1)}, f32[768,256]{1,0:T(8,128)S(1)}) custom-call(s32[4,4]{1,0:T(4,128)S(1)} %copy.28.scal_ref, s32[8,4480]{1,0:T(8,128)S(1)} %broadcast_in_dim.2.ids_ref, bf16[4096,4096]{1,0:T(8,128)(2,1)} %bitcast.21, bf16[4096,256]{1,0:T(8,128)(2,1)S(1)} %get-tuple-element.90.samples_ref, ...), custom_call_target="tpu_custom_call" | custom-call | flops 3355443200 | bytes 13107200 | tf_op jit(solution)/shard_map/sketch/pallas_call | solution.py:123
  136.8 4.4 %collective-permute-start.19 = (f32[768,128]{1,0:T(8,128)S(1)}, f32[768,128]{1,0:T(8,128)S(1)}, u32[]{:S(2)}, u32[]{:S(2)}) collective-permute-start(f32[768,128]{1,0:T(8,128)S(1)} %get-tuple-element.52), channel_id=1, source_target_pairs={{0,1},{3,2},{4,5},{7,6},{8,9},{11,10},{12,13},{15,14},{16,17},{19,... | collective-permute-start | bytes 1179656 | tf_op jit(solution)/shard_map/ppermute | solution.py:204
  144.1 6.2 %collective-permute-done.19 = f32[768,128]{1,0:T(8,128)S(1)} collective-permute-done((f32[768,128]{1,0:T(8,128)S(1)}, f32[768,128]{1,0:T(8,128)S(1)}, u32[]{:S(2)}, u32[]{:S(2)}) %collective-permute-start.19) | collective-permute-done | bytes 393248 | tf_op jit(solution)/shard_map/ppermute | solution.py:204
  151.0 8.9 %sketch.15 = (f32[768,256]{1,0:T(8,128)S(1)}, f32[768,256]{1,0:T(8,128)}) custom-call(s32[4,4]{1,0:T(4,128)S(1)} %copy.29.scal_ref, s32[8,4480]{1,0:T(8,128)S(1)} %broadcast_in_dim.2.ids_ref, bf16[4096,4096]{1,0:T(8,128)(2,1)} %bitcast.22, bf16[4096,256]{1,0:T(8,128)(2,1)S(1)} %get-tuple-element.90.samples_ref, f32[768,128]{1,0:T(8,128)S(1)} %collective-permute-done.26.rest_0_), custom_call_target="tpu_custom_call" | custom-call | flops 3355443200 | bytes 13107200 | tf_op jit(solution)/shard_map/sketch/pallas_call | solution.py:123
  160.0 5.3 %collective-permute-start.15 = (f32[128,256]{1,0:T(8,128)S(1)}, f32[128,256]{1,0:T(8,128)S(1)}, u32[]{:S(2)}, u32[]{:S(2)}) collective-permute-start(f32[128,256]{1,0:T(8,128)S(1)} %dynamic-slice_add_fusion), channel_id=1, source_target_pairs={{0,1},{1,0},{2,3},{3,2},{4,5},{5,4},{6,7},{7,6},{8,9},{9,8},{10,11... | collective-permute-start | bytes 393224 | tf_op jit(solution)/shard_map/ppermute | solution.py:204
  168.9 8.9 %sketch.13 = (f32[768,256]{1,0:T(8,128)S(1)}, f32[768,256]{1,0:T(8,128)}) custom-call(s32[4,4]{1,0:T(4,128)S(1)} %copy.26.scal_ref, s32[8,4480]{1,0:T(8,128)S(1)} %broadcast_in_dim.2.ids_ref, bf16[4096,4096]{1,0:T(8,128)(2,1)} %bitcast.23, bf16[4096,256]{1,0:T(8,128)(2,1)S(1)} %get-tuple-element.90.samples_ref, f32[768,128]{1,0:T(8,128)S(1)} %collective-permute-done.20.rest_0_), custom_call_target="tpu_custom_call" | custom-call | flops 3355443200 | bytes 13107200 | tf_op jit(solution)/shard_map/sketch/pallas_call | solution.py:123
  179.0 8.2 %collective-permute-done.16 = f32[128,256]{1,0:T(8,128)S(1)} collective-permute-done((f32[128,256]{1,0:T(8,128)S(1)}, f32[128,256]{1,0:T(8,128)S(1)}, u32[]{:S(2)}, u32[]{:S(2)}) %collective-permute-start.16) | collective-permute-done | bytes 131104 | tf_op jit(solution)/shard_map/ppermute | solution.py:204
  193.6 8.9 %inverse_factor.1 = f32[256,256]{1,0:T(8,128)S(1)} custom-call(f32[256,256]{1,0:T(8,128)S(1)} %maximum_multiply_fusion.gram_ref), custom_call_target="tpu_custom_call" | custom-call | tf_op jit(solution)/shard_map/inverse_factor/pallas_call | solution.py:189
  203.5 3.5 %collective-permute-start.28 = (f32[768,128]{1,0:T(8,128)S(1)}, f32[768,128]{1,0:T(8,128)S(1)}, u32[]{:S(2)}, u32[]{:S(2)}) collective-permute-start(f32[768,128]{1,0:T(8,128)S(1)} %add.327), channel_id=1, source_target_pairs={{0,1},{1,0},{2,3},{3,2},{4,5},{5,4},{6,7},{7,6},{8,9},{9,8},{10,11... | collective-permute-start | bytes 1179656 | tf_op jit(solution)/shard_map/ppermute | solution.py:204
  208.7 7.4 %collective-permute-done.28 = f32[768,128]{1,0:T(8,128)S(1)} collective-permute-done((f32[768,128]{1,0:T(8,128)S(1)}, f32[768,128]{1,0:T(8,128)S(1)}, u32[]{:S(2)}, u32[]{:S(2)}) %collective-permute-start.28) | collective-permute-done | bytes 393248 | tf_op jit(solution)/shard_map/ppermute | solution.py:204
  229.0 2.9 %collective-permute-done.31 = f32[128,128]{1,0:T(8,128)S(1)} collective-permute-done((f32[128,128]{1,0:T(8,128)S(1)}, f32[128,128]{1,0:T(8,128)S(1)}, u32[]{:S(2)}, u32[]{:S(2)}) %collective-permute-start.31) | collective-permute-done | bytes 65568 | tf_op jit(solution)/shard_map/ppermute | solution.py:204
  (168 shorter events, 65.6 us)
Async XLA Ops:
  34.0 14.1 %collective-permute-start.7 = (f32[768,128]{1,0:T(8,128)S(1)}, f32[768,128]{1,0:T(8,128)S(1)}, u32[]{:S(2)}, u32[]{:S(2)}) collective-permute-start(f32[768,128]{1,0:T(8,128)S(1)} %get-tuple-element.40.rest_0_), channel_id=1, source_target_pairs={{0,1},{3,2},{4,5},{7,6},{8,9},{11,10},{12,13},{15,14},{16,17},{19,... | collective-permute-start | bytes 1179656 | tf_op jit(solution)/shard_map/ppermute | solution.py:204
  38.7 17.8 %collective-permute-start.1 = (f32[768,128]{1,0:T(8,128)S(1)}, f32[768,128]{1,0:T(8,128)S(1)}, u32[]{:S(2)}, u32[]{:S(2)}) collective-permute-start(f32[768,128]{1,0:T(8,128)S(1)} %get-tuple-element.36), channel_id=1, source_target_pairs={{0,1},{3,2},{4,5},{7,6},{8,9},{11,10},{12,13},{15,14},{16,17},{19,... | collective-permute-start | bytes 1179656 | tf_op jit(solution)/shard_map/ppermute | solution.py:204
  40.8 23.5 %collective-permute-start.5 = (f32[768,128]{1,0:T(8,128)S(1)}, f32[768,128]{1,0:T(8,128)}, u32[]{:S(2)}, u32[]{:S(2)}) collective-permute-start(f32[768,128]{1,0:T(8,128)S(1)} %get-tuple-element.43), channel_id=1, source_target_pairs={{0,1},{3,2},{4,5},{7,6},{8,9},{11,10},{12,13},{15,14},{16,17},{19,... | collective-permute-start | bytes 1179656 | tf_op jit(solution)/shard_map/ppermute | solution.py:204
  48.9 17.3 %collective-permute-start.8 = (f32[768,128]{1,0:T(8,128)}, f32[768,128]{1,0:T(8,128)S(1)}, u32[]{:S(2)}, u32[]{:S(2)}) collective-permute-start(f32[768,128]{1,0:T(8,128)} %add.299), channel_id=1, source_target_pairs={{1,2},{2,1},{5,6},{6,5},{9,10},{10,9},{13,14},{14,13},{17,18},{18,... | collective-permute-start | bytes 1179656 | tf_op jit(solution)/shard_map/ppermute | solution.py:204
  57.3 20.2 %collective-permute-start.2 = (f32[768,128]{1,0:T(8,128)}, f32[768,128]{1,0:T(8,128)S(1)}, u32[]{:S(2)}, u32[]{:S(2)}) collective-permute-start(f32[768,128]{1,0:T(8,128)} %add.292), channel_id=1, source_target_pairs={{1,2},{2,1},{5,6},{6,5},{9,10},{10,9},{13,14},{14,13},{17,18},{18,... | collective-permute-start | bytes 1179656 | tf_op jit(solution)/shard_map/ppermute | solution.py:204
  65.4 29.5 %collective-permute-start.6 = (f32[768,128]{1,0:T(8,128)S(1)}, f32[768,128]{1,0:T(8,128)S(1)}, u32[]{:S(2)}, u32[]{:S(2)}) collective-permute-start(f32[768,128]{1,0:T(8,128)S(1)} %add.297), channel_id=1, source_target_pairs={{1,2},{2,1},{5,6},{6,5},{9,10},{10,9},{13,14},{14,13},{17,18},{18,... | collective-permute-start | bytes 1179656 | tf_op jit(solution)/shard_map/ppermute | solution.py:204
  77.5 29.2 %collective-permute-start.9 = (f32[768,256]{1,0:T(8,128)}, f32[768,256]{1,0:T(8,128)}, u32[]{:S(2)}, u32[]{:S(2)}) collective-permute-start(f32[768,256]{1,0:T(8,128)} %get-tuple-element.45), channel_id=1, source_target_pairs={{0,16},{16,0},{1,17},{17,1},{2,18},{18,2},{3,19},{19,3},{4,20},{20... | collective-permute-start | bytes 2359304 | tf_op jit(solution)/shard_map/ppermute | solution.py:270
  86.3 24.4 %collective-permute-start.3 = (f32[768,256]{1,0:T(8,128)}, f32[768,256]{1,0:T(8,128)}, u32[]{:S(2)}, u32[]{:S(2)}) collective-permute-start(f32[768,256]{1,0:T(8,128)} %get-tuple-element.38), channel_id=1, source_target_pairs={{0,16},{16,0},{1,17},{17,1},{2,18},{18,2},{3,19},{19,3},{4,20},{20... | collective-permute-start | bytes 2359304 | tf_op jit(solution)/shard_map/ppermute | solution.py:270
  86.9 17.8 %collective-permute-start.11 = (f32[768,128]{1,0:T(8,128)}, f32[768,128]{1,0:T(8,128)}, u32[]{:S(2)}, u32[]{:S(2)}) collective-permute-start(f32[768,128]{1,0:T(8,128)} %get-tuple-element.48), channel_id=1, source_target_pairs={{0,1},{3,2},{4,5},{7,6},{8,9},{11,10},{12,13},{15,14},{16,17},{19,... | collective-permute-start | bytes 1179656 | tf_op jit(solution)/shard_map/ppermute | solution.py:204
  106.0 36.2 %collective-permute-start.12 = (f32[768,128]{1,0:T(8,128)S(1)}, f32[768,128]{1,0:T(8,128)S(1)}, u32[]{:S(2)}, u32[]{:S(2)}) collective-permute-start(f32[768,128]{1,0:T(8,128)S(1)} %add.304), channel_id=1, source_target_pairs={{1,2},{2,1},{5,6},{6,5},{9,10},{10,9},{13,14},{14,13},{17,18},{18,... | collective-permute-start | bytes 1179656 | tf_op jit(solution)/shard_map/ppermute | solution.py:204
  108.2 34.0 %collective-permute-start.13 = (f32[768,128]{1,0:T(8,128)S(1)}, f32[768,128]{1,0:T(8,128)S(1)}, u32[]{:S(2)}, u32[]{:S(2)}) collective-permute-start(f32[768,128]{1,0:T(8,128)S(1)} %add.306), channel_id=1, source_target_pairs={{0,1},{1,0},{2,3},{3,2},{4,5},{5,4},{6,7},{7,6},{8,9},{9,8},{10,11... | collective-permute-start | bytes 1179656 | tf_op jit(solution)/shard_map/ppermute | solution.py:204
  110.7 18.0 %collective-permute-start.10 = (f32[768,128]{1,0:T(8,128)S(1)}, f32[768,128]{1,0:T(8,128)S(1)}, u32[]{:S(2)}, u32[]{:S(2)}) collective-permute-start(f32[768,128]{1,0:T(8,128)S(1)} %add.302), channel_id=1, source_target_pairs={{0,1},{1,0},{2,3},{3,2},{4,5},{5,4},{6,7},{7,6},{8,9},{9,8},{10,11... | collective-permute-start | bytes 1179656 | tf_op jit(solution)/shard_map/ppermute | solution.py:204
  113.2 28.0 %collective-permute-start.25 = (f32[768,128]{1,0:T(8,128)S(1)}, f32[768,128]{1,0:T(8,128)S(1)}, u32[]{:S(2)}, u32[]{:S(2)}) collective-permute-start(f32[768,128]{1,0:T(8,128)S(1)} %get-tuple-element.59), channel_id=1, source_target_pairs={{0,1},{3,2},{4,5},{7,6},{8,9},{11,10},{12,13},{15,14},{16,17},{19,... | collective-permute-start | bytes 1179656 | tf_op jit(solution)/shard_map/ppermute | solution.py:204
  136.7 28.6 %collective-permute-start.22 = (f32[768,256]{1,0:T(8,128)S(1)}, f32[768,256]{1,0:T(8,128)S(1)}, u32[]{:S(2)}, u32[]{:S(2)}) collective-permute-start(f32[768,256]{1,0:T(8,128)S(1)} %get-tuple-element.57), channel_id=1, source_target_pairs={{0,16},{16,0},{1,17},{17,1},{2,18},{18,2},{3,19},{19,3},{4,20},{20... | collective-permute-start | bytes 2359304 | tf_op jit(solution)/shard_map/ppermute | solution.py:270
  136.8 13.4 %collective-permute-start.19 = (f32[768,128]{1,0:T(8,128)S(1)}, f32[768,128]{1,0:T(8,128)S(1)}, u32[]{:S(2)}, u32[]{:S(2)}) collective-permute-start(f32[768,128]{1,0:T(8,128)S(1)} %get-tuple-element.52), channel_id=1, source_target_pairs={{0,1},{3,2},{4,5},{7,6},{8,9},{11,10},{12,13},{15,14},{16,17},{19,... | collective-permute-start | bytes 1179656 | tf_op jit(solution)/shard_map/ppermute | solution.py:204
  143.8 16.1 %collective-permute-start.14 = (f32[128,256]{1,0:T(8,128)S(1)}, f32[128,256]{1,0:T(8,128)S(1)}, u32[]{:S(2)}, u32[]{:S(2)}) collective-permute-start(f32[128,256]{1,0:T(8,128)S(1)} %constant_dynamic-slice_fusion.2), channel_id=1, source_target_pairs={{0,16},{16,0},{1,17},{17,1},{2,18},{18,2},{3,19},{19,3},{4,20},{20... | collective-permute-start | bytes 393224 | tf_op jit(solution)/shard_map/ppermute | solution.py:229
  150.3 18.7 %collective-permute-start.20 = (f32[768,128]{1,0:T(8,128)S(1)}, f32[768,128]{1,0:T(8,128)S(1)}, u32[]{:S(2)}, u32[]{:S(2)}) collective-permute-start(f32[768,128]{1,0:T(8,128)S(1)} %add.317), channel_id=1, source_target_pairs={{1,2},{2,1},{5,6},{6,5},{9,10},{10,9},{13,14},{14,13},{17,18},{18,... | collective-permute-start | bytes 1179656 | tf_op jit(solution)/shard_map/ppermute | solution.py:204
  159.8 31.0 %collective-permute-start.27 = (f32[768,256]{1,0:T(8,128)}, f32[768,256]{1,0:T(8,128)}, u32[]{:S(2)}, u32[]{:S(2)}) collective-permute-start(f32[768,256]{1,0:T(8,128)} %get-tuple-element.61), channel_id=1, source_target_pairs={{0,16},{16,0},{1,17},{17,1},{2,18},{18,2},{3,19},{19,3},{4,20},{20... | collective-permute-start | bytes 2359304 | tf_op jit(solution)/shard_map/ppermute | solution.py:270
  160.0 18.9 %collective-permute-start.15 = (f32[128,256]{1,0:T(8,128)S(1)}, f32[128,256]{1,0:T(8,128)S(1)}, u32[]{:S(2)}, u32[]{:S(2)}) collective-permute-start(f32[128,256]{1,0:T(8,128)S(1)} %dynamic-slice_add_fusion), channel_id=1, source_target_pairs={{0,1},{1,0},{2,3},{3,2},{4,5},{5,4},{6,7},{7,6},{8,9},{9,8},{10,11... | collective-permute-start | bytes 393224 | tf_op jit(solution)/shard_map/ppermute | solution.py:204
  166.2 22.8 %collective-permute-start.33 = (f32[768,128]{1,0:T(8,128)}, f32[768,128]{1,0:T(8,128)}, u32[]{:S(2)}, u32[]{:S(2)}) collective-permute-start(f32[768,128]{1,0:T(8,128)} %get-tuple-element.64), channel_id=1, source_target_pairs={{0,1},{3,2},{4,5},{7,6},{8,9},{11,10},{12,13},{15,14},{16,17},{19,... | collective-permute-start | bytes 1179656 | tf_op jit(solution)/shard_map/ppermute | solution.py:204
  178.7 28.4 %collective-permute-start.21 = (f32[768,256]{1,0:T(8,128)}, f32[768,256]{1,0:T(8,128)S(1)}, u32[]{:S(2)}, u32[]{:S(2)}) collective-permute-start(f32[768,256]{1,0:T(8,128)} %get-tuple-element.54), channel_id=1, source_target_pairs={{0,16},{16,0},{1,17},{17,1},{2,18},{18,2},{3,19},{19,3},{4,20},{20... | collective-permute-start | bytes 2359304 | tf_op jit(solution)/shard_map/ppermute | solution.py:270
  187.3 15.2 %collective-permute-start.23 = (f32[768,128]{1,0:T(8,128)}, f32[768,128]{1,0:T(8,128)S(1)}, u32[]{:S(2)}, u32[]{:S(2)}) collective-permute-start(f32[768,128]{1,0:T(8,128)} %get-tuple-element.58), channel_id=1, source_target_pairs={{0,1},{3,2},{4,5},{7,6},{8,9},{11,10},{12,13},{15,14},{16,17},{19,... | collective-permute-start | bytes 1179656 | tf_op jit(solution)/shard_map/ppermute | solution.py:204
  190.2 17.0 %collective-permute-start.34 = (f32[768,128]{1,0:T(8,128)S(1)}, f32[768,128]{1,0:T(8,128)S(1)}, u32[]{:S(2)}, u32[]{:S(2)}) collective-permute-start(f32[768,128]{1,0:T(8,128)S(1)} %add.332), channel_id=1, source_target_pairs={{1,2},{2,1},{5,6},{6,5},{9,10},{10,9},{13,14},{14,13},{17,18},{18,... | collective-permute-start | bytes 1179656 | tf_op jit(solution)/shard_map/ppermute | solution.py:204
  192.4 14.8 %collective-permute-start.35 = (f32[768,128]{1,0:T(8,128)S(1)}, f32[768,128]{1,0:T(8,128)S(1)}, u32[]{:S(2)}, u32[]{:S(2)}) collective-permute-start(f32[768,128]{1,0:T(8,128)S(1)} %add.334), channel_id=1, source_target_pairs={{0,1},{1,0},{2,3},{3,2},{4,5},{5,4},{6,7},{7,6},{8,9},{9,8},{10,11... | collective-permute-start | bytes 1179656 | tf_op jit(solution)/shard_map/ppermute | solution.py:204
  (31 other events, 229.4 us)

commit v2 on v0

v2 whole, which is shorter than its diff:
```python
import functools

import jax
import jax.numpy as jnp
import numpy as np
from jax import lax
from jax.experimental import pallas as pl
from jax.experimental.pallas import tpu as pltpu
from jax.sharding import PartitionSpec as P

NP = 24576
K = 256
HI = lax.Precision.HIGHEST
CORES = [(0, 1), (1, 0)]
MIB = 1024 * 1024
LIGHT = pl.CostEstimate(flops=0, bytes_accessed=0, transcendentals=0)


def sample_rows(seed_value, parents, sample_width):
    hashed = (
        parents[:, None] * 40503
        + lax.iota(jnp.int32, sample_width)[None, :] * 9973
        + seed_value * 2654435
    )
    hashed = hashed ^ hashed >> 15 & 131071
    hashed = hashed * 73244475
    hashed = hashed ^ hashed >> 13 & 524287
    hashed = hashed * 1274126177
    hashed = hashed ^ hashed >> 16 & 65535
    unit_value = (hashed & 16777215).astype(jnp.float32) * (1.0 / 16777216.0)
    return (unit_value - 0.5) * 3.4641016


DEPTH = 3


def row_chunk(rows):
    return rows // 8 if rows % 128 == 0 else rows


def tile_sizes(own_rows, block_rows):
    tile = max(d for d in range(8, min(own_rows, 240) + 1, 8) if own_rows % d == 0)
    return tile, min(256, block_rows)


def tile_scalars(row_ids, bases, own_rows):
    block_rows = row_ids.shape[0]
    tile, reach = tile_sizes(own_rows, block_rows)
    starts = bases[:, None] + lax.iota(jnp.int32, own_rows // tile)[None, :] * tile
    before = jnp.sum((row_ids[None, None, :] < starts[:, :, None]).astype(jnp.int32), axis=2)
    return jnp.concatenate([bases[:, None], jnp.minimum(before // 16 * 16, block_rows - reach)], axis=1)


def multiply(step, steps, first, schur_ref, samples_ref, held, sems):
    chunk = held.shape[1]

    def copy(s):
        slot = lax.rem(s, DEPTH)
        start = pl.multiple_of(first + s * chunk, 16)
        return pltpu.make_async_copy(schur_ref.at[pl.ds(start, chunk), :], held.at[slot], sems.at[slot])

    @pl.when(step == 0)
    def _():
        for s in range(min(DEPTH - 1, steps)):
            copy(s).start()

    @pl.when(step + DEPTH - 1 < steps)
    def _():
        copy(step + DEPTH - 1).start()

    copy(step).wait()
    value = jnp.dot(held[lax.rem(step, DEPTH)], samples_ref[...], preferred_element_type=jnp.float32)
    high = value.astype(jnp.bfloat16)
    return high, (value - high.astype(jnp.float32)).astype(jnp.bfloat16)


def spread(block, scal_ref, ids_ref, high_ref, low_ref, out_ref):
    tile, reach = tile_sizes(out_ref.shape[0], high_ref.shape[0])
    for i in range(out_ref.shape[0] // tile):
        child = pl.multiple_of(scal_ref[block, 1 + i], 16)
        lane = pl.multiple_of(child // 128 * 128, 128)
        ids = pltpu.roll(ids_ref[:, pl.ds(lane, 384)], lax.rem(384 - (child - lane), 384), 1)
        ids = jnp.broadcast_to(ids[0:1, :reach], (tile, reach))
        wanted = scal_ref[block, 0] + i * tile + lax.broadcasted_iota(jnp.int32, (tile, reach), 0)
        select = (ids == wanted).astype(jnp.float32).astype(jnp.bfloat16)
        out_ref[i * tile : (i + 1) * tile, :] = jnp.dot(
            select, high_ref[pl.ds(child, reach), :], preferred_element_type=jnp.float32
        ) + jnp.dot(select, low_ref[pl.ds(child, reach), :], preferred_element_type=jnp.float32)


def multiply_kernel(steps, schur_ref, samples_ref, high_ref, low_ref, held, sems):
    high_ref[...], low_ref[...] = multiply(pl.program_id(0), steps, 0, schur_ref, samples_ref, held, sems)


def sketch_kernel(steps, heads, scal_ref, ids_ref, schur_ref, samples_ref, *refs):
    head_refs = refs[:heads]
    mine_ref, first_ref, rest_ref, held, high, low, sems = refs[heads:]
    step = pl.program_id(0)
    chunk = held.shape[1]
    done = high.shape[0] - steps * chunk
    block = step - steps
    even = lax.rem(block, 2) == 0

    if heads:

        @pl.when(step == 0)
        def _():
            high[:done, :] = head_refs[0][...]
            low[:done, :] = head_refs[1][...]

    @pl.when(step < steps)
    def _():
        rows = pl.ds(pl.multiple_of(done + step * chunk, 16), chunk)
        high[rows, :], low[rows, :] = multiply(step, steps, done, schur_ref, samples_ref, held, sems)

    for chosen, out_ref in ((block == 0, first_ref), (even & (block > 0), rest_ref), (~even & (block > 0), mine_ref)):

        @pl.when(chosen)
        def _(out_ref=out_ref):
            spread(block, scal_ref, ids_ref, high, low, out_ref)


VMEM = pl.BlockSpec(memory_space=pltpu.VMEM)


def multiply_rows(child_block, samples, rows):
    block_rows, block_cols = child_block.shape
    width = samples.shape[1]
    chunk = row_chunk(block_rows)
    return pl.pallas_call(
        functools.partial(multiply_kernel, rows // chunk),
        out_shape=[jax.ShapeDtypeStruct((rows, width), jnp.bfloat16)] * 2,
        grid=(rows // chunk,),
        in_specs=[pl.BlockSpec(memory_space=pl.ANY), VMEM],
        out_specs=[pl.BlockSpec((chunk, width), lambda s: (s, 0))] * 2,
        scratch_shapes=[
            pltpu.VMEM((DEPTH, chunk, block_cols), jnp.bfloat16),
            pltpu.SemaphoreType.DMA((DEPTH,)),
        ],
        compiler_params=pltpu.CompilerParams(vmem_limit_bytes=24 * MIB),
        cost_estimate=LIGHT,
        name="multiply",
    )(child_block, samples)


def sketch(scalars, ids, child_block, samples, own_rows, heads=()):
    block_rows, block_cols = child_block.shape
    width = samples.shape[1]
    chunk = row_chunk(block_rows)
    steps = (block_rows - (heads[0].shape[0] if heads else 0)) // chunk
    pairs = scalars.shape[0] // 2

    def output(count, skipped):
        shape = jax.ShapeDtypeStruct((count * own_rows, width), jnp.float32)
        index = lambda s, _: (jnp.clip((s - steps) // 2 - skipped, 0, count - 1), 0)
        return shape, pl.BlockSpec((own_rows, width), index)

    shapes, specs = zip(output(pairs, 0), output(1, 0), output(pairs - 1, 1))
    return pl.pallas_call(
        functools.partial(sketch_kernel, steps, len(heads)),
        out_shape=shapes,
        grid_spec=pltpu.PrefetchScalarGridSpec(
            num_scalar_prefetch=1,
            grid=(steps + scalars.shape[0],),
            in_specs=[VMEM, pl.BlockSpec(memory_space=pl.ANY), VMEM] + [VMEM] * len(heads),
            out_specs=specs,
            scratch_shapes=[
                pltpu.VMEM((DEPTH, chunk, block_cols), jnp.bfloat16),
                pltpu.VMEM((block_rows, width), jnp.bfloat16),
                pltpu.VMEM((block_rows, width), jnp.bfloat16),
                pltpu.SemaphoreType.DMA((DEPTH,)),
            ],
        ),
        compiler_params=pltpu.CompilerParams(vmem_limit_bytes=32 * MIB),
        cost_estimate=LIGHT,
        name="sketch",
    )(scalars, ids, child_block, samples, *heads)


def eliminate(tiles, size):
    count = size // 8
    sub = lax.broadcasted_iota(jnp.int32, (8, size), 0)
    lane = lax.broadcasted_iota(jnp.int32, (8, size), 1)
    rows = list(tiles)
    inverse = [(lane == sub + 8 * t).astype(jnp.float32) for t in range(count)]

    def row(value, k):
        return jnp.broadcast_to(value[k : k + 1, :], (8, size))

    for t in range(count):
        columns = [
            [jnp.broadcast_to(rows[i][:, 8 * t + k : 8 * t + k + 1], (8, size)) for k in range(8)]
            for i in range(t, count)
        ]
        diagonal = jnp.ones((8, size), jnp.float32)
        for k in range(8):
            pivot = row(columns[0][k], k)
            scale = 1.0 / pivot
            diagonal = jnp.where(sub == k, pivot, diagonal)
            heads = [row(columns[0][l], k) * scale for l in range(k + 1, 8)]
            head_row = row(rows[t], k) * scale
            head_inv = row(inverse[t], k) * scale
            for i in range(t, count):
                factor = columns[i - t][k]
                if i == t:
                    factor = jnp.where(sub > k, factor, 0.0)
                for l in range(k + 1, 8):
                    columns[i - t][l] = columns[i - t][l] - factor * heads[l - k - 1]
                rows[i] = rows[i] - factor * head_row
                inverse[i] = inverse[i] - factor * head_inv
        inverse[t] = inverse[t] * lax.rsqrt(diagonal)
    return jnp.concatenate(inverse, axis=0)


def factor_kernel(gram_ref, out_ref):
    half = gram_ref.shape[0] // 2

    def dot(a, b, dims):
        return lax.dot_general(a, b, (dims, ((), ())), precision=HI, preferred_element_type=jnp.float32)

    first = eliminate([gram_ref[8 * t : 8 * t + 8, :half] for t in range(half // 8)], half)
    lower = dot(gram_ref[half:, :half], first, ((1,), (1,)))
    rest = gram_ref[half:, half:] - dot(lower, lower, ((1,), (1,)))
    second = eliminate([rest[8 * t : 8 * t + 8, :] for t in range(half // 8)], half)
    out_ref[:half, :half] = first
    out_ref[:half, half:] = jnp.zeros((half, half), jnp.float32)
    out_ref[half:, :half] = -dot(second, dot(lower, first, ((1,), (0,))), ((1,), (0,)))
    out_ref[half:, half:] = second


def inverse_factor(gram):
    return pl.pallas_call(
        factor_kernel,
        out_shape=jax.ShapeDtypeStruct(gram.shape, jnp.float32),
        compiler_params=pltpu.CompilerParams(vmem_limit_bytes=16 * MIB),
        cost_estimate=LIGHT,
        name="inverse_factor",
    )(gram)


ORDER = np.array([[3, 2, 1, 0], [3, 2, 0, 1], [0, 1, 3, 2], [0, 1, 2, 3]], np.int32)
INWARD = [(0, 1), (3, 2)]
ACROSS = [(1, 2), (2, 1)]
PAIRS = [(0, 1), (1, 0), (2, 3), (3, 2)]
CROSSED = [(0, 2), (2, 0), (1, 3), (3, 1)]


def hop(value, pairs):
    return lax.ppermute(value, "col", pairs)


def fence(*values):
    return lax.optimization_barrier(values)


def add_kernel(widths, *refs):
    refs = list(refs)
    outs = refs[sum(len(w) for w in widths[:-1]) :]
    terms = []
    for w in widths[:-1]:
        terms.append((refs[: len(w)], w))
        refs = refs[len(w) :]

    def columns(parts, low, high):
        start = 0
        for ref, width in zip(*parts):
            if start <= low and high <= start + width:
                return ref[:, low - start : high - start]
            start += width

    cuts = sorted({sum(w[:i]) for w in widths for i in range(len(w) + 1)})
    for low, high in zip(cuts, cuts[1:]):
        value = sum(columns(term, low, high) for term in terms)
        start = 0
        for ref, width in zip(outs, widths[-1]):
            if start <= low and high <= start + width:
                ref[:, low - start : high - start] = value
            start += width


def add(terms, parts, rows=None, places=None):
    rows = rows or terms[0][0].shape[0]
    places = places or [0] * len(terms)
    width = sum(part.shape[1] for part in terms[0])
    widths = [[part.shape[1] for part in term] for term in terms] + [[width // parts] * parts]
    specs = [
        pl.BlockSpec((rows, part.shape[1]), lambda s, place=place: (place, 0))
        for term, place in zip(terms, places)
        for part in term
    ]
    return pl.pallas_call(
        functools.partial(add_kernel, widths),
        out_shape=[jax.ShapeDtypeStruct((rows, width // parts), jnp.float32)] * parts,
        grid=(1,),
        in_specs=specs,
        out_specs=[pl.BlockSpec((rows, width // parts), lambda s: (0, 0))] * parts,
        compiler_params=pltpu.CompilerParams(vmem_limit_bytes=16 * MIB),
        cost_estimate=LIGHT,
        name="add",
    )(*[part for term in terms for part in term])


def plus(*terms):
    return add([[term] for term in terms], 1)[0]


def core_sum(value, child_index):
    half = value.shape[0] // 2
    mine = lax.dynamic_slice_in_dim(value, child_index * half, half)
    other = lax.dynamic_slice_in_dim(value, (1 - child_index) * half, half)
    return mine + lax.ppermute(other, "child", CORES)


def core_join(mine, child_index):
    other = lax.ppermute(mine, "child", CORES)
    low = jnp.where(child_index == 0, mine, other)
    high = jnp.where(child_index == 0, other, mine)
    return jnp.concatenate([low, high], axis=0)


def times_transposed(a, b):
    return lax.dot_general(a, b, (((1,), (1,)), ((), ())), precision=HI)


def body(schur_blocks, child_map, round_seeds):
    child_block = schur_blocks[0]
    block_rows, block_cols = child_block.shape
    child_count = lax.axis_size("child")
    col_count = lax.axis_size("col")
    row_count = lax.axis_size("row")
    child_index = lax.axis_index("child")
    row_index = lax.axis_index("row")
    col_index = lax.axis_index("col")
    own_map = lax.dynamic_index_in_dim(child_map, child_index, 0, keepdims=False)
    col_ids = lax.dynamic_slice_in_dim(own_map, col_index * block_cols, block_cols)
    row_ids = lax.dynamic_slice_in_dim(own_map, row_index * block_rows, block_rows)
    leaf_rows = NP // row_count
    own_rows = leaf_rows // (child_count * col_count)
    leaf_base = row_index * leaf_rows
    ids = jnp.broadcast_to(jnp.pad(row_ids, (0, 384), constant_values=-1)[None, :], (8, block_rows + 384))

    def sampled(r, ids):
        return sample_rows(round_seeds[r], ids, K).astype(jnp.bfloat16)

    if child_count == 2 and col_count == len(ORDER):
        places = lax.dynamic_index_in_dim(jnp.asarray(ORDER), col_index, 0, keepdims=False)
        turns = jnp.stack([1 - child_index, child_index])
        bases = leaf_base + (turns[None, :] * col_count + places[:, None]) * own_rows
        scalars = tile_scalars(row_ids, bases.reshape(-1), own_rows)

        def swap(value):
            return lax.ppermute(value, "child", CORES)

        def part(mine, rest, p):
            return add([[mine], [rest]], 1, own_rows, [p, p - 1])[0]

        mine, first, rest = sketch(scalars, ids, child_block, sampled(0, col_ids), own_rows)
        own0 = add([[mine], [swap(first)]], 2, own_rows)
        *own0, rest, late_ids = fence(*own0, rest, col_ids)

        in3 = [hop(half, INWARD) for half in own0]
        rest = swap(rest)
        samples, own1 = fence(sampled(1, late_ids), part(mine, rest, 1))
        in2 = hop(own1, INWARD)
        heads = multiply_rows(child_block, samples, block_rows // 4 * 3)
        own2, own3 = part(mine, rest, 2), part(mine, rest, 3)
        in3[0], own0[0], *heads = fence(in3[0], own0[0], *heads)
        mid1 = [hop(plus(own0[0], in3[0]), ACROSS)]
        in3[1], own0[1], *heads = fence(in3[1], own0[1], *heads)
        mid1 += [hop(plus(own0[1], in3[1]), ACROSS)]
        later = sketch(scalars, ids, child_block, samples, own_rows, heads)
        out1 = add([[own2], mid1], 1)[0]
        in2, out1, own1, own3, mine, first, rest = fence(in2, out1, own1, own3, *later)

        last = hop(out1, PAIRS)
        mid2 = hop(plus(own1, in2), ACROSS)
        own0 = list(add([[mine], [swap(first)]], 2, own_rows))
        in3 = [hop(half, INWARD) for half in own0]
        rest = swap(rest)
        own1, own2, own3_next = [part(mine, rest, p) for p in (1, 2, 3)]
        first_leaf = plus(plus(own3, last), mid2)
        first_leaf, own1, own2, own3 = fence(first_leaf, own1, own2, own3_next)
        in2 = hop(own1, INWARD)
        gram = lax.dot_general(first_leaf, first_leaf, (((0,), (0,)), ((), ())), precision=HI)
        gram = core_sum(gram, child_index)
        in3[0], own0[0], gram = fence(in3[0], own0[0], gram)
        mid1 = [hop(plus(own0[0], in3[0]), ACROSS)]
        in3[1], own0[1], gram = fence(in3[1], own0[1], gram)
        mid1 += [hop(plus(own0[1], in3[1]), ACROSS)]
        gram = gram + hop(gram, INWARD)
        out1 = add([[own2], mid1], 1)[0]
        in2, out1, own1, gram = fence(in2, out1, own1, gram)

        last = hop(out1, PAIRS)
        gram = gram + hop(gram, ACROSS)
        mid2 = hop(plus(own1, in2), ACROSS)
        second, gram = fence(plus(plus(own3, last), mid2), gram)
        cross = core_sum(jnp.dot(first_leaf.T, second, precision=HI), child_index)
        arrived = hop(jnp.concatenate([cross, gram], axis=0), PAIRS)
        cross = cross + arrived[: K // 2]
        edge = (col_index == 0) | (col_index == col_count - 1)
        gram = jnp.where(edge, arrived[K // 2 :], gram)
        cross = cross + hop(cross, CROSSED)
        inverse = inverse_factor(core_join(gram, child_index) / leaf_rows)
        leaf_basis = times_transposed(first_leaf, inverse)
        dual = jnp.dot(leaf_basis, inverse, precision=HI)
        cross, leaf_basis, dual = fence(cross, leaf_basis, dual)
        cross = core_join(cross, child_index) / leaf_rows
    else:
        bases = leaf_base + lax.iota(jnp.int32, child_count * col_count) * own_rows
        scalars = tile_scalars(row_ids, bases, own_rows)

        def leaf(r):
            odd, *even = sketch(scalars, ids, child_block, sampled(r, col_ids), own_rows)
            even = jnp.concatenate(even, axis=0)
            blocks = jnp.stack([even.reshape(-1, own_rows, K), odd.reshape(-1, own_rows, K)], axis=1)
            return lax.psum_scatter(
                blocks.reshape(leaf_rows, K), ("child", "col"), scatter_dimension=0, tiled=True
            )

        first_leaf = leaf(0)
        second = leaf(1)
        gram = lax.psum(jnp.dot(first_leaf.T, first_leaf, precision=HI), ("child", "col")) / leaf_rows
        inverse = inverse_factor(gram)
        cross = lax.psum(jnp.dot(first_leaf.T, second, precision=HI), ("child", "col")) / leaf_rows
        leaf_basis = times_transposed(first_leaf, inverse)
        dual = jnp.dot(leaf_basis, inverse, precision=HI)

    return (leaf_basis, second - jnp.dot(dual, cross, precision=HI))


def solution(mesh):
    placed = (P("child", "row", "col"), P(), P())
    return jax.shard_map(
        body,
        mesh=mesh,
        in_specs=placed,
        out_specs=(P(("row", "child", "col"), None), P(("row", "child", "col"), None)),
        check_vma=False,
    )
```

time: 495 us -> 180 us (0.36)
  waiting for transfers between devices: 242 us -> 46.8 us
  local copies, waits for them, and re-layouts: 104 us -> 4.17 us
  matrix products: 73.2 us -> 6.11 us
  Pallas kernels: 0 us -> 63.2 us
  other arithmetic: 57.8 us -> 5.67 us
  starting transfers between devices: 0.34 us -> 50.3 us
  between operations: 16.6 us -> 2.55 us
    reduce_scatter x2 -> x0, waiting for transfers between devices: 145 us -> none  [extend(): lax.psum_scatter(pieces.reshape(own_rows * lax.axis_size(('child', 'col')...]
    psum x2 -> x0, waiting for transfers between devices: 97 us -> none  [the longest x1 54.3 us: body(): coefficients = lax.psum(coef_local, ('child', 'col')) / leaf_rows]
    gather x4 -> x0, local copies, waits for them, and re-layouts: 86.2 us -> none  [the longest x2 51.9 us: extend(): values = jnp.take(partial_value, positions, axis=0)]
    dot_general x7 -> x5, matrix products: 70.9 us -> 6.11 us  [the longest x1 1.67 us: body(): return (leaf_basis, second - jnp.dot(dual, cross, precision=HI))]
    pallas_call x0 -> x24, Pallas kernels: none -> 63.2 us  [the longest x2 28.9 us: sketch(): pl.pallas_call(functools.partial(sketch_kernel, steps, len(heads)), out_s...]
    another operation x11 -> x0, other arithmetic: 54.4 us -> none  [the longest x7 34.6 us: body(): lower_factor = jnp.linalg.cholesky(gram_matrix)]
    ppermute x0 -> x26, starting transfers between devices: none -> 50.3 us  [the longest x18 48.4 us: hop(): return lax.ppermute(value, 'col', pairs)]
    ppermute x0 -> x26, waiting for transfers between devices: none -> 46.8 us  [the longest x18 41 us: hop(): return lax.ppermute(value, 'col', pairs)]
  transfers between devices with their start and end apart: 4 -> 26, of which waited for: 4 -> 10; matrix products, arithmetic and copies ran while one was open for 26% -> 3% of each run, Pallas kernels for 0% -> 26%
where the time goes in v2:
time: 180 us; the launch traced here: 179 us
  Pallas kernels  63.2 us (35%)
  starting transfers between devices  50.3 us (28%)
  waiting for transfers between devices  46.8 us (26%)
  matrix products  6.11 us (3%)
  other arithmetic  5.67 us (3%)
  local copies, waits for them, and re-layouts  4.17 us (2%)
  between operations  2.55 us (1%)
    ppermute x18, starting transfers between devices, hop(): return lax.ppermute(value, 'col', pairs)  48.4 us
    ppermute x18, waiting for transfers between devices, hop(): return lax.ppermute(value, 'col', pairs)  41 us
    pallas_call x2, Pallas kernels, sketch(): pl.pallas_call(functools.partial(sketch_kernel, steps, len(heads)), out_s...  28.9 us
    pallas_call x20, Pallas kernels, add(): pl.pallas_call(functools.partial(add_kernel, widths), out_shape=[jax.Shap...  15.5 us
    pallas_call x1, Pallas kernels, multiply_rows(): pl.pallas_call(functools.partial(multiply_kernel, rows // chunk), out_sha...  9.94 us
    pallas_call x1, Pallas kernels, inverse_factor(): pl.pallas_call(factor_kernel, out_shape=jax.ShapeDtypeStruct(gram.shape,...  8.93 us
    convert_element_type x2, other arithmetic, sampled(): return sample_rows(round_seeds[r], ids, K).astype(jnp.bfloat16)  4.88 us
  transfers between devices with their start and end apart: 26, of which 10 were waited for; matrix products, arithmetic and copies ran while one was open for 3% of the time, Pallas kernels for 26%

profile of v2, /device:TPU:0, one launch (start us, length us, event | category | flops | bytes accessed | tf_op | source)
XLA Modules:
  0.0 178.8 jit_solution(16374578298451062589)
XLA Ops:
  5.1 2.4 %multiply_convert_fusion.1.samples_ref = bf16[4096,256]{1,0:T(8,128)(2,1)S(1)} fusion(s32[]{:T(128)} %bitcast.6, s32[256]{0:T(256)S(1)} %iota_multiply_fusion, s32[4096]{0:T(1024)S(1)} %broadcast_multiply_fusion.1), kind=kLoop, calls=%fused_computation.1 | loop fusion | flops 19922944 | bytes 2114564 | tf_op jit(solution)/shard_map/convert_element_type | solution.py:343
  7.6 17.2 %sketch.2 = (f32[3072,256]{1,0:T(8,128)S(1)}, f32[768,256]{1,0:T(8,128)S(1)}, f32[2304,256]{1,0:T(8,128)S(1)}) custom-call(s32[8,5]{1,0:T(8,128)S(1)} %pad_add_fusion.scal_ref, s32[8,4480]{1,0:T(8,128)S(1)} %broadcast_in_dim.4.ids_ref, bf16[4096,4096]{1,0:T(8,128)(2,1)} %bitcast.18, bf16[4096,256]{1,0:T(8,128)(2,1)S(1)} %multiply_convert_fusion.1.samples_ref), custom_call_target="tpu_custom_call" | custom-call | tf_op jit(solution)/shard_map/sketch/pallas_call | solution.py:159
  25.3 1.9 %collective-permute-done.refs_1_ = f32[768,256]{1,0:T(8,128)S(1)} collective-permute-done((f32[768,256]{1,0:T(8,128)S(1)}, f32[768,256]{1,0:T(8,128)S(1)}, u32[]{:S(2)}, u32[]{:S(2)}) %collective-permute-start) | collective-permute-done | bytes 786464 | tf_op jit(solution)/shard_map/ppermute | solution.py:352
  28.4 4.7 %collective-permute-start.3 = (f32[768,128]{1,0:T(8,128)S(1)}, f32[768,128]{1,0:T(8,128)S(1)}, u32[]{:S(2)}, u32[]{:S(2)}) collective-permute-start(f32[768,128]{1,0:T(8,128)S(1)} %get-tuple-element.66.refs_0_), channel_id=1, source_target_pairs={{0,1},{3,2},{4,5},{7,6},{8,9},{11,10},{12,13},{15,14},{16,17},{19,... | collective-permute-start | bytes 1179656 | tf_op jit(solution)/shard_map/ppermute | solution.py:249
  34.4 2.4 %multiply_convert_fusion.samples_ref = bf16[4096,256]{1,0:T(8,128)(2,1)S(1)} fusion(s32[]{:T(128)} %bitcast.7, s32[4096]{0:T(1024)S(1)} %broadcast_multiply_fusion, s32[256]{0:T(256)S(1)} %iota_multiply_fusion), kind=kLoop, calls=%fused_computation | loop fusion | flops 19922944 | bytes 2114564 | tf_op jit(solution)/shard_map/convert_element_type | solution.py:343
  38.3 9.9 %multiply.3 = (bf16[3072,256]{1,0:T(8,128)(2,1)S(1)}, bf16[3072,256]{1,0:T(8,128)(2,1)S(1)}) custom-call(bf16[4096,4096]{1,0:T(8,128)(2,1)} %bitcast.19, bf16[4096,256]{1,0:T(8,128)(2,1)S(1)} %multiply_convert_fusion.samples_ref), custom_call_target="tpu_custom_call" | custom-call | tf_op jit(solution)/shard_map/multiply/pallas_call | solution.py:130
  49.0 1.9 %collective-permute-done.5.refs_1_ = f32[768,128]{1,0:T(8,128)S(1)} collective-permute-done((f32[768,128]{1,0:T(8,128)S(1)}, f32[768,128]{1,0:T(8,128)S(1)}, u32[]{:S(2)}, u32[]{:S(2)}) %collective-permute-start.5) | collective-permute-done | bytes 393248 | tf_op jit(solution)/shard_map/ppermute | solution.py:249
  51.6 11.7 %sketch.3 = (f32[3072,256]{1,0:T(8,128)S(1)}, f32[768,256]{1,0:T(8,128)}, f32[2304,256]{1,0:T(8,128)}) custom-call(s32[8,5]{1,0:T(8,128)S(1)} %pad_add_fusion.scal_ref, s32[8,4480]{1,0:T(8,128)S(1)} %broadcast_in_dim.4.ids_ref, bf16[4096,4096]{1,0:T(8,128)(2,1)} %bitcast.20, bf16[4096,256]{1,0:T(8,128)(2,1)S(1)} %multiply_convert_fusion.samples_ref, ...), custom_call_target="tpu_custom_call" | custom-call | tf_op jit(solution)/shard_map/sketch/pallas_call | solution.py:159
  64.7 2.5 %collective-permute-done.2.refs_1_ = f32[768,256]{1,0:T(8,128)S(1)} collective-permute-done((f32[768,256]{1,0:T(8,128)S(1)}, f32[768,256]{1,0:T(8,128)S(1)}, u32[]{:S(2)}, u32[]{:S(2)}) %collective-permute-start.2) | collective-permute-done | bytes 786464 | tf_op jit(solution)/shard_map/ppermute | solution.py:249
  67.7 3.1 %collective-permute-start.7 = (f32[768,256]{1,0:T(8,128)}, f32[768,256]{1,0:T(8,128)}, u32[]{:S(2)}, u32[]{:S(2)}) collective-permute-start(f32[768,256]{1,0:T(8,128)} %add.232), channel_id=1, source_target_pairs={{0,1},{1,0},{2,3},{3,2},{4,5},{5,4},{6,7},{7,6},{8,9},{9,8},{10,11... | collective-permute-start | bytes 2359304 | tf_op jit(solution)/shard_map/ppermute | solution.py:249
  73.3 2.0 %add.240 = (f32[768,128]{1,0:T(8,128)}, f32[768,128]{1,0:T(8,128)S(1)}) custom-call(f32[3072,256]{1,0:T(8,128)S(1)} %get-tuple-element.82.refs_0_, f32[768,256]{1,0:T(8,128)} %collective-permute-done.11.refs_1_), custom_call_target="tpu_custom_call" | custom-call | tf_op jit(solution)/shard_map/add/pallas_call | solution.py:291
  75.3 5.6 %collective-permute-start.12 = (f32[768,128]{1,0:T(8,128)}, f32[768,128]{1,0:T(8,128)}, u32[]{:S(2)}, u32[]{:S(2)}) collective-permute-start(f32[768,128]{1,0:T(8,128)} %get-tuple-element.90.refs_0_), channel_id=1, source_target_pairs={{0,1},{3,2},{4,5},{7,6},{8,9},{11,10},{12,13},{15,14},{16,17},{19,... | collective-permute-start | bytes 1179656 | tf_op jit(solution)/shard_map/ppermute | solution.py:249
  80.9 2.1 %collective-permute-start.15 = (f32[768,128]{1,0:T(8,128)S(1)}, f32[768,128]{1,0:T(8,128)}, u32[]{:S(2)}, u32[]{:S(2)}) collective-permute-start(f32[768,128]{1,0:T(8,128)S(1)} %get-tuple-element.94.refs_0_), channel_id=1, source_target_pairs={{0,1},{3,2},{4,5},{7,6},{8,9},{11,10},{12,13},{15,14},{16,17},{19,... | collective-permute-start | bytes 1179656 | tf_op jit(solution)/shard_map/ppermute | solution.py:249
  83.0 6.0 %collective-permute-done.7.refs_1_ = f32[768,256]{1,0:T(8,128)} collective-permute-done((f32[768,256]{1,0:T(8,128)}, f32[768,256]{1,0:T(8,128)}, u32[]{:S(2)}, u32[]{:S(2)}) %collective-permute-start.7) | collective-permute-done | bytes 786464 | tf_op jit(solution)/shard_map/ppermute | solution.py:249
  91.5 2.4 %add.237.refs_0_ = f32[768,256]{1,0:T(8,128)} custom-call(f32[3072,256]{1,0:T(8,128)S(1)} %get-tuple-element.82.refs_0_, f32[2304,256]{1,0:T(8,128)} %collective-permute-done.9.refs_1_), custom_call_target="tpu_custom_call" | custom-call | tf_op jit(solution)/shard_map/add/pallas_call | solution.py:291
  97.2 5.2 %collective-permute-start.10 = (f32[768,256]{1,0:T(8,128)}, f32[768,256]{1,0:T(8,128)S(1)}, u32[]{:S(2)}, u32[]{:S(2)}) collective-permute-start(f32[768,256]{1,0:T(8,128)} %add.237.refs_0_), channel_id=1, source_target_pairs={{0,1},{3,2},{4,5},{7,6},{8,9},{11,10},{12,13},{15,14},{16,17},{19,... | collective-permute-start | bytes 2359304 | tf_op jit(solution)/shard_map/ppermute | solution.py:249
  109.0 5.7 %collective-permute-start.17 = (f32[128,256]{1,0:T(8,128)S(1)}, f32[128,256]{1,0:T(8,128)S(1)}, u32[]{:S(2)}, u32[]{:S(2)}) collective-permute-start(f32[128,256]{1,0:T(8,128)S(1)} %dynamic-slice_add_fusion.1), channel_id=1, source_target_pairs={{0,1},{3,2},{4,5},{7,6},{8,9},{11,10},{12,13},{15,14},{16,17},{19,... | collective-permute-start | bytes 393224 | tf_op jit(solution)/shard_map/ppermute | solution.py:249
  114.7 9.7 %collective-permute-done.17 = f32[128,256]{1,0:T(8,128)S(1)} collective-permute-done((f32[128,256]{1,0:T(8,128)S(1)}, f32[128,256]{1,0:T(8,128)S(1)}, u32[]{:S(2)}, u32[]{:S(2)}) %collective-permute-start.17) | collective-permute-done | bytes 131104 | tf_op jit(solution)/shard_map/ppermute | solution.py:249
  124.6 2.9 %collective-permute-start.18 = (f32[768,256]{1,0:T(8,128)S(1)}, f32[768,256]{1,0:T(8,128)S(1)}, u32[]{:S(2)}, u32[]{:S(2)}) collective-permute-start(f32[768,256]{1,0:T(8,128)S(1)} %add.243), channel_id=1, source_target_pairs={{0,1},{1,0},{2,3},{3,2},{4,5},{5,4},{6,7},{7,6},{8,9},{9,8},{10,11... | collective-permute-start | bytes 2359304 | tf_op jit(solution)/shard_map/ppermute | solution.py:249
  130.4 14.2 %collective-permute-done.18.refs_1_ = f32[768,256]{1,0:T(8,128)S(1)} collective-permute-done((f32[768,256]{1,0:T(8,128)S(1)}, f32[768,256]{1,0:T(8,128)S(1)}, u32[]{:S(2)}, u32[]{:S(2)}) %collective-permute-start.18) | collective-permute-done | bytes 786464 | tf_op jit(solution)/shard_map/ppermute | solution.py:249
  147.7 7.8 %collective-permute-start.22 = (f32[256,256]{1,0:T(8,128)S(1)}, f32[256,256]{1,0:T(8,128)S(1)}, u32[]{:S(2)}, u32[]{:S(2)}) collective-permute-start(f32[256,256]{1,0:T(8,128)S(1)} %pad_maximum_fusion), channel_id=1, source_target_pairs={{0,1},{1,0},{2,3},{3,2},{4,5},{5,4},{6,7},{7,6},{8,9},{9,8},{10,11... | collective-permute-start | bytes 786440 | tf_op jit(solution)/shard_map/ppermute | solution.py:249
  155.5 6.6 %collective-permute-done.22 = f32[256,256]{1,0:T(8,128)S(1)} collective-permute-done((f32[256,256]{1,0:T(8,128)S(1)}, f32[256,256]{1,0:T(8,128)S(1)}, u32[]{:S(2)}, u32[]{:S(2)}) %collective-permute-start.22) | collective-permute-done | bytes 262176 | tf_op jit(solution)/shard_map/ppermute | solution.py:249
  162.3 2.8 %collective-permute-start.23 = (f32[128,256]{1,0:T(8,128)S(1)}, f32[128,256]{1,0:T(8,128)S(1)}, u32[]{:S(2)}, u32[]{:S(2)}) collective-permute-start(f32[128,256]{1,0:T(8,128)S(1)} %get-tuple-element.111), channel_id=1, source_target_pairs={{0,2},{2,0},{1,3},{3,1},{4,6},{6,4},{5,7},{7,5},{8,10},{10,8},{9,1... | collective-permute-start | bytes 393224 | tf_op jit(solution)/shard_map/ppermute | solution.py:249
  165.1 8.9 %inverse_factor.1 = f32[256,256]{1,0:T(8,128)S(1)} custom-call(f32[256,256]{1,0:T(8,128)S(1)} %maximum_multiply_fusion.gram_ref), custom_call_target="tpu_custom_call" | custom-call | tf_op jit(solution)/shard_map/inverse_factor/pallas_call | solution.py:232
  (107 shorter events, 36.5 us)
Async XLA Ops:
  24.8 2.4 %collective-permute-start = (f32[768,256]{1,0:T(8,128)S(1)}, f32[768,256]{1,0:T(8,128)S(1)}, u32[]{:S(2)}, u32[]{:S(2)}) collective-permute-start(f32[768,256]{1,0:T(8,128)S(1)} %get-tuple-element.55), channel_id=1, source_target_pairs={{0,16},{16,0},{1,17},{17,1},{2,18},{18,2},{3,19},{19,3},{4,20},{20... | collective-permute-start | bytes 2359304 | tf_op jit(solution)/shard_map/ppermute | solution.py:352
  27.3 9.5 %collective-permute-start.1 = (f32[2304,256]{1,0:T(8,128)S(1)}, f32[2304,256]{1,0:T(8,128)S(1)}, u32[]{:S(2)}, u32[]{:S(2)}) collective-permute-start(f32[2304,256]{1,0:T(8,128)S(1)} %get-tuple-element.60), channel_id=1, source_target_pairs={{0,16},{16,0},{1,17},{17,1},{2,18},{18,2},{3,19},{19,3},{4,20},{20... | collective-permute-start | bytes 7077896 | tf_op jit(solution)/shard_map/ppermute | solution.py:352
  28.4 19.8 %collective-permute-start.3 = (f32[768,128]{1,0:T(8,128)S(1)}, f32[768,128]{1,0:T(8,128)S(1)}, u32[]{:S(2)}, u32[]{:S(2)}) collective-permute-start(f32[768,128]{1,0:T(8,128)S(1)} %get-tuple-element.66.refs_0_), channel_id=1, source_target_pairs={{0,1},{3,2},{4,5},{7,6},{8,9},{11,10},{12,13},{15,14},{16,17},{19,... | collective-permute-start | bytes 1179656 | tf_op jit(solution)/shard_map/ppermute | solution.py:249
  33.0 17.8 %collective-permute-start.5 = (f32[768,128]{1,0:T(8,128)S(1)}, f32[768,128]{1,0:T(8,128)S(1)}, u32[]{:S(2)}, u32[]{:S(2)}) collective-permute-start(f32[768,128]{1,0:T(8,128)S(1)} %get-tuple-element.71.refs_0_), channel_id=1, source_target_pairs={{0,1},{3,2},{4,5},{7,6},{8,9},{11,10},{12,13},{15,14},{16,17},{19,... | collective-permute-start | bytes 1179656 | tf_op jit(solution)/shard_map/ppermute | solution.py:249
  36.9 30.2 %collective-permute-start.2 = (f32[768,256]{1,0:T(8,128)S(1)}, f32[768,256]{1,0:T(8,128)S(1)}, u32[]{:S(2)}, u32[]{:S(2)}) collective-permute-start(f32[768,256]{1,0:T(8,128)S(1)} %add.228.refs_0_), channel_id=1, source_target_pairs={{0,1},{3,2},{4,5},{7,6},{8,9},{11,10},{12,13},{15,14},{16,17},{19,... | collective-permute-start | bytes 2359304 | tf_op jit(solution)/shard_map/ppermute | solution.py:249
  48.3 15.2 %collective-permute-start.4 = (f32[768,128]{1,0:T(8,128)S(1)}, f32[768,128]{1,0:T(8,128)S(1)}, u32[]{:S(2)}, u32[]{:S(2)}) collective-permute-start(f32[768,128]{1,0:T(8,128)S(1)} %add.230), channel_id=1, source_target_pairs={{1,2},{2,1},{5,6},{6,5},{9,10},{10,9},{13,14},{14,13},{17,18},{18,... | collective-permute-start | bytes 1179656 | tf_op jit(solution)/shard_map/ppermute | solution.py:249
  50.9 12.6 %collective-permute-start.6 = (f32[768,128]{1,0:T(8,128)S(1)}, f32[768,128]{1,0:T(8,128)S(1)}, u32[]{:S(2)}, u32[]{:S(2)}) collective-permute-start(f32[768,128]{1,0:T(8,128)S(1)} %add.231), channel_id=1, source_target_pairs={{1,2},{2,1},{5,6},{6,5},{9,10},{10,9},{13,14},{14,13},{17,18},{18,... | collective-permute-start | bytes 1179656 | tf_op jit(solution)/shard_map/ppermute | solution.py:249
  67.2 24.3 %collective-permute-start.9 = (f32[2304,256]{1,0:T(8,128)}, f32[2304,256]{1,0:T(8,128)}, u32[]{:S(2)}, u32[]{:S(2)}) collective-permute-start(f32[2304,256]{1,0:T(8,128)} %get-tuple-element.83), channel_id=1, source_target_pairs={{0,16},{16,0},{1,17},{17,1},{2,18},{18,2},{3,19},{19,3},{4,20},{20... | collective-permute-start | bytes 7077896 | tf_op jit(solution)/shard_map/ppermute | solution.py:352
  67.2 6.1 %collective-permute-start.11 = (f32[768,256]{1,0:T(8,128)}, f32[768,256]{1,0:T(8,128)}, u32[]{:S(2)}, u32[]{:S(2)}) collective-permute-start(f32[768,256]{1,0:T(8,128)} %get-tuple-element.88), channel_id=1, source_target_pairs={{0,16},{16,0},{1,17},{17,1},{2,18},{18,2},{3,19},{19,3},{4,20},{20... | collective-permute-start | bytes 2359304 | tf_op jit(solution)/shard_map/ppermute | solution.py:352
  67.7 21.3 %collective-permute-start.7 = (f32[768,256]{1,0:T(8,128)}, f32[768,256]{1,0:T(8,128)}, u32[]{:S(2)}, u32[]{:S(2)}) collective-permute-start(f32[768,256]{1,0:T(8,128)} %add.232), channel_id=1, source_target_pairs={{0,1},{1,0},{2,3},{3,2},{4,5},{5,4},{6,7},{7,6},{8,9},{9,8},{10,11... | collective-permute-start | bytes 2359304 | tf_op jit(solution)/shard_map/ppermute | solution.py:249
  71.8 18.5 %collective-permute-start.8 = (f32[768,256]{1,0:T(8,128)}, f32[768,256]{1,0:T(8,128)}, u32[]{:S(2)}, u32[]{:S(2)}) collective-permute-start(f32[768,256]{1,0:T(8,128)} %add.235), channel_id=1, source_target_pairs={{1,2},{2,1},{5,6},{6,5},{9,10},{10,9},{13,14},{14,13},{17,18},{18,... | collective-permute-start | bytes 2359304 | tf_op jit(solution)/shard_map/ppermute | solution.py:249
  75.3 30.1 %collective-permute-start.12 = (f32[768,128]{1,0:T(8,128)}, f32[768,128]{1,0:T(8,128)}, u32[]{:S(2)}, u32[]{:S(2)}) collective-permute-start(f32[768,128]{1,0:T(8,128)} %get-tuple-element.90.refs_0_), channel_id=1, source_target_pairs={{0,1},{3,2},{4,5},{7,6},{8,9},{11,10},{12,13},{15,14},{16,17},{19,... | collective-permute-start | bytes 1179656 | tf_op jit(solution)/shard_map/ppermute | solution.py:249
  80.9 26.3 %collective-permute-start.15 = (f32[768,128]{1,0:T(8,128)S(1)}, f32[768,128]{1,0:T(8,128)}, u32[]{:S(2)}, u32[]{:S(2)}) collective-permute-start(f32[768,128]{1,0:T(8,128)S(1)} %get-tuple-element.94.refs_0_), channel_id=1, source_target_pairs={{0,1},{3,2},{4,5},{7,6},{8,9},{11,10},{12,13},{15,14},{16,17},{19,... | collective-permute-start | bytes 1179656 | tf_op jit(solution)/shard_map/ppermute | solution.py:249
  97.2 27.4 %collective-permute-start.10 = (f32[768,256]{1,0:T(8,128)}, f32[768,256]{1,0:T(8,128)S(1)}, u32[]{:S(2)}, u32[]{:S(2)}) collective-permute-start(f32[768,256]{1,0:T(8,128)} %add.237.refs_0_), channel_id=1, source_target_pairs={{0,1},{3,2},{4,5},{7,6},{8,9},{11,10},{12,13},{15,14},{16,17},{19,... | collective-permute-start | bytes 2359304 | tf_op jit(solution)/shard_map/ppermute | solution.py:249
  103.9 1.4 collective-permute-start.13
  106.6 17.9 %collective-permute-start.14 = (f32[768,128]{1,0:T(8,128)S(1)}, f32[768,128]{1,0:T(8,128)S(1)}, u32[]{:S(2)}, u32[]{:S(2)}) collective-permute-start(f32[768,128]{1,0:T(8,128)S(1)} %add.241), channel_id=1, source_target_pairs={{1,2},{2,1},{5,6},{6,5},{9,10},{10,9},{13,14},{14,13},{17,18},{18,... | collective-permute-start | bytes 1179656 | tf_op jit(solution)/shard_map/ppermute | solution.py:249
  108.3 16.2 %collective-permute-start.16 = (f32[768,128]{1,0:T(8,128)S(1)}, f32[768,128]{1,0:T(8,128)S(1)}, u32[]{:S(2)}, u32[]{:S(2)}) collective-permute-start(f32[768,128]{1,0:T(8,128)S(1)} %add.242), channel_id=1, source_target_pairs={{1,2},{2,1},{5,6},{6,5},{9,10},{10,9},{13,14},{14,13},{17,18},{18,... | collective-permute-start | bytes 1179656 | tf_op jit(solution)/shard_map/ppermute | solution.py:249
  109.0 15.5 %collective-permute-start.17 = (f32[128,256]{1,0:T(8,128)S(1)}, f32[128,256]{1,0:T(8,128)S(1)}, u32[]{:S(2)}, u32[]{:S(2)}) collective-permute-start(f32[128,256]{1,0:T(8,128)S(1)} %dynamic-slice_add_fusion.1), channel_id=1, source_target_pairs={{0,1},{3,2},{4,5},{7,6},{8,9},{11,10},{12,13},{15,14},{16,17},{19,... | collective-permute-start | bytes 393224 | tf_op jit(solution)/shard_map/ppermute | solution.py:249
  124.6 19.9 %collective-permute-start.18 = (f32[768,256]{1,0:T(8,128)S(1)}, f32[768,256]{1,0:T(8,128)S(1)}, u32[]{:S(2)}, u32[]{:S(2)}) collective-permute-start(f32[768,256]{1,0:T(8,128)S(1)} %add.243), channel_id=1, source_target_pairs={{0,1},{1,0},{2,3},{3,2},{4,5},{5,4},{6,7},{7,6},{8,9},{9,8},{10,11... | collective-permute-start | bytes 2359304 | tf_op jit(solution)/shard_map/ppermute | solution.py:249
  128.8 15.9 %collective-permute-start.19 = (f32[768,256]{1,0:T(8,128)S(1)}, f32[768,256]{1,0:T(8,128)S(1)}, u32[]{:S(2)}, u32[]{:S(2)}) collective-permute-start(f32[768,256]{1,0:T(8,128)S(1)} %add.245), channel_id=1, source_target_pairs={{1,2},{2,1},{5,6},{6,5},{9,10},{10,9},{13,14},{14,13},{17,18},{18,... | collective-permute-start | bytes 2359304 | tf_op jit(solution)/shard_map/ppermute | solution.py:249
  146.2 1.4 collective-permute-start.21
  147.7 14.5 %collective-permute-start.22 = (f32[256,256]{1,0:T(8,128)S(1)}, f32[256,256]{1,0:T(8,128)S(1)}, u32[]{:S(2)}, u32[]{:S(2)}) collective-permute-start(f32[256,256]{1,0:T(8,128)S(1)} %pad_maximum_fusion), channel_id=1, source_target_pairs={{0,1},{1,0},{2,3},{3,2},{4,5},{5,4},{6,7},{7,6},{8,9},{9,8},{10,11... | collective-permute-start | bytes 786440 | tf_op jit(solution)/shard_map/ppermute | solution.py:249
  162.2 2.8 %collective-permute-start.24 = (f32[128,256]{1,0:T(8,128)S(1)}, f32[128,256]{1,0:T(8,128)S(1)}, u32[]{:S(2)}, u32[]{:S(2)}) collective-permute-start(f32[128,256]{1,0:T(8,128)S(1)} %get-tuple-element.110), channel_id=1, source_target_pairs={{0,16},{16,0},{1,17},{17,1},{2,18},{18,2},{3,19},{19,3},{4,20},{20... | collective-permute-start | bytes 393224 | tf_op jit(solution)/shard_map/ppermute | solution.py:315
  162.3 13.4 %collective-permute-start.23 = (f32[128,256]{1,0:T(8,128)S(1)}, f32[128,256]{1,0:T(8,128)S(1)}, u32[]{:S(2)}, u32[]{:S(2)}) collective-permute-start(f32[128,256]{1,0:T(8,128)S(1)} %get-tuple-element.111), channel_id=1, source_target_pairs={{0,2},{2,0},{1,3},{3,1},{4,6},{6,4},{5,7},{7,5},{8,10},{10,8},{9,1... | collective-permute-start | bytes 393224 | tf_op jit(solution)/shard_map/ppermute | solution.py:249
  (11 other events, 136.7 us)

commit v3 on v2

--- a/solution.py
+++ b/solution.py
@@ -31,7 +31,7 @@
     return (unit_value - 0.5) * 3.4641016
 
 
-DEPTH = 3
+DEPTH = 4
 
 
 def row_chunk(rows):
@@ -78,7 +78,7 @@
     tile, reach = tile_sizes(out_ref.shape[0], high_ref.shape[0])
     for i in range(out_ref.shape[0] // tile):
         child = pl.multiple_of(scal_ref[block, 1 + i], 16)
-        lane = pl.multiple_of(child // 128 * 128, 128)
+        lane = pl.multiple_of(jnp.minimum(child // 128 * 128, ids_ref.shape[1] - 384), 128)
         ids = pltpu.roll(ids_ref[:, pl.ds(lane, 384)], lax.rem(384 - (child - lane), 384), 1)
         ids = jnp.broadcast_to(ids[0:1, :reach], (tile, reach))
         wanted = scal_ref[block, 0] + i * tile + lax.broadcasted_iota(jnp.int32, (tile, reach), 0)
@@ -98,8 +98,7 @@
     step = pl.program_id(0)
     chunk = held.shape[1]
     done = high.shape[0] - steps * chunk
-    block = step - steps
-    even = lax.rem(block, 2) == 0
+    place = step - steps
 
     if heads:
 
@@ -113,10 +112,14 @@
         rows = pl.ds(pl.multiple_of(done + step * chunk, 16), chunk)
         high[rows, :], low[rows, :] = multiply(step, steps, done, schur_ref, samples_ref, held, sems)
 
-    for chosen, out_ref in ((block == 0, first_ref), (even & (block > 0), rest_ref), (~even & (block > 0), mine_ref)):
+    for chosen, out_ref, block in (
+        (place == 0, first_ref, 0),
+        (place > 0, rest_ref, 2 * place),
+        (place >= 0, mine_ref, 2 * place + 1),
+    ):
 
         @pl.when(chosen)
-        def _(out_ref=out_ref):
+        def _(out_ref=out_ref, block=block):
             spread(block, scal_ref, ids_ref, high, low, out_ref)
 
 
@@ -137,7 +140,7 @@
             pltpu.VMEM((DEPTH, chunk, block_cols), jnp.bfloat16),
             pltpu.SemaphoreType.DMA((DEPTH,)),
         ],
-        compiler_params=pltpu.CompilerParams(vmem_limit_bytes=24 * MIB),
+        compiler_params=pltpu.CompilerParams(vmem_limit_bytes=32 * MIB),
         cost_estimate=LIGHT,
         name="multiply",
     )(child_block, samples)
@@ -152,7 +155,7 @@
 
     def output(count, skipped):
         shape = jax.ShapeDtypeStruct((count * own_rows, width), jnp.float32)
-        index = lambda s, _: (jnp.clip((s - steps) // 2 - skipped, 0, count - 1), 0)
+        index = lambda s, _: (jnp.clip(s - steps - skipped, 0, count - 1), 0)
         return shape, pl.BlockSpec((own_rows, width), index)
 
     shapes, specs = zip(output(pairs, 0), output(1, 0), output(pairs - 1, 1))
@@ -161,7 +164,7 @@
         out_shape=shapes,
         grid_spec=pltpu.PrefetchScalarGridSpec(
             num_scalar_prefetch=1,
-            grid=(steps + scalars.shape[0],),
+            grid=(steps + pairs,),
             in_specs=[VMEM, pl.BlockSpec(memory_space=pl.ANY), VMEM] + [VMEM] * len(heads),
             out_specs=specs,
             scratch_shapes=[
@@ -171,7 +174,7 @@
                 pltpu.SemaphoreType.DMA((DEPTH,)),
             ],
         ),
-        compiler_params=pltpu.CompilerParams(vmem_limit_bytes=32 * MIB),
+        compiler_params=pltpu.CompilerParams(vmem_limit_bytes=40 * MIB),
         cost_estimate=LIGHT,
         name="sketch",
     )(scalars, ids, child_block, samples, *heads)
@@ -241,6 +244,7 @@
 ORDER = np.array([[3, 2, 1, 0], [3, 2, 0, 1], [0, 1, 3, 2], [0, 1, 2, 3]], np.int32)
 INWARD = [(0, 1), (3, 2)]
 ACROSS = [(1, 2), (2, 1)]
+OUTWARD = [(1, 0), (2, 3)]
 PAIRS = [(0, 1), (1, 0), (2, 3), (3, 2)]
 CROSSED = [(0, 2), (2, 0), (1, 3), (3, 1)]
 
@@ -331,13 +335,12 @@
     child_index = lax.axis_index("child")
     row_index = lax.axis_index("row")
     col_index = lax.axis_index("col")
-    own_map = lax.dynamic_index_in_dim(child_map, child_index, 0, keepdims=False)
-    col_ids = lax.dynamic_slice_in_dim(own_map, col_index * block_cols, block_cols)
-    row_ids = lax.dynamic_slice_in_dim(own_map, row_index * block_rows, block_rows)
+    col_ids = lax.dynamic_slice(child_map, (child_index, col_index * block_cols), (1, block_cols))[0]
+    row_ids = lax.dynamic_slice(child_map, (child_index, row_index * block_rows), (1, block_rows))[0]
     leaf_rows = NP // row_count
     own_rows = leaf_rows // (child_count * col_count)
     leaf_base = row_index * leaf_rows
-    ids = jnp.broadcast_to(jnp.pad(row_ids, (0, 384), constant_values=-1)[None, :], (8, block_rows + 384))
+    ids = jnp.broadcast_to(row_ids[None, :], (8, block_rows))
 
     def sampled(r, ids):
         return sample_rows(round_seeds[r], ids, K).astype(jnp.bfloat16)
@@ -394,12 +397,12 @@
         last = hop(out1, PAIRS)
         gram = gram + hop(gram, ACROSS)
         mid2 = hop(plus(own1, in2), ACROSS)
-        second, gram = fence(plus(plus(own3, last), mid2), gram)
+        second = plus(plus(own3, last), mid2)
         cross = core_sum(jnp.dot(first_leaf.T, second, precision=HI), child_index)
-        arrived = hop(jnp.concatenate([cross, gram], axis=0), PAIRS)
-        cross = cross + arrived[: K // 2]
         edge = (col_index == 0) | (col_index == col_count - 1)
-        gram = jnp.where(edge, arrived[K // 2 :], gram)
+        gram = jnp.where(edge, hop(gram, OUTWARD), gram)
+        cross = cross + hop(cross, PAIRS)
+        cross, gram = fence(cross, gram)
         cross = cross + hop(cross, CROSSED)
         inverse = inverse_factor(core_join(gram, child_index) / leaf_rows)
         leaf_basis = times_transposed(first_leaf, inverse)

time: 180 us -> 177 us (0.983)
  starting transfers between devices: 50.3 us -> 47.9 us
    ppermute x18 -> x19, starting transfers between devices: 48.4 us -> 46 us  [hop(): return lax.ppermute(value, 'col', pairs)]
    ppermute x18 -> x19, waiting for transfers between devices: 41 us -> 42 us  [hop(): return lax.ppermute(value, 'col', pairs)]
  transfers between devices with their start and end apart: 26 -> 27, of which waited for: 10 -> 11; matrix products, arithmetic and copies ran while one was open for 3% -> 4% of each run, Pallas kernels for 26% -> 26%
where the time goes in v3:
time: 177 us; the launch traced here: 176 us
  Pallas kernels  62.2 us (35%)
  starting transfers between devices  47.9 us (27%)
  waiting for transfers between devices  47.2 us (27%)
  matrix products  6.11 us (3%)
  other arithmetic  5.66 us (3%)
  local copies, waits for them, and re-layouts  4.16 us (2%)
  between operations  2.57 us (1%)
    ppermute x19, starting transfers between devices, hop(): return lax.ppermute(value, 'col', pairs)  46 us
    ppermute x19, waiting for transfers between devices, hop(): return lax.ppermute(value, 'col', pairs)  42 us
    pallas_call x2, Pallas kernels, sketch(): pl.pallas_call(functools.partial(sketch_kernel, steps, len(heads)), out_s...  27.8 us
    pallas_call x20, Pallas kernels, add(): pl.pallas_call(functools.partial(add_kernel, widths), out_shape=[jax.Shap...  15.5 us
    pallas_call x1, Pallas kernels, multiply_rows(): pl.pallas_call(functools.partial(multiply_kernel, rows // chunk), out_sha...  9.99 us
    pallas_call x1, Pallas kernels, inverse_factor(): pl.pallas_call(factor_kernel, out_shape=jax.ShapeDtypeStruct(gram.shape,...  8.93 us
    convert_element_type x2, other arithmetic, sampled(): return sample_rows(round_seeds[r], ids, K).astype(jnp.bfloat16)  4.88 us
  transfers between devices with their start and end apart: 27, of which 11 were waited for; matrix products, arithmetic and copies ran while one was open for 4% of the time, Pallas kernels for 26%

profile of v3, /device:TPU:0, one launch (start us, length us, event | category | flops | bytes accessed | tf_op | source)
XLA Modules:
  0.0 175.8 jit_solution(4954779915753441429)
XLA Ops:
  5.1 2.4 %multiply_convert_fusion.1.samples_ref = bf16[4096,256]{1,0:T(8,128)(2,1)S(1)} fusion(s32[]{:T(128)} %bitcast.6, s32[256]{0:T(256)S(1)} %iota_multiply_fusion, s32[4096]{0:T(1024)S(1)} %broadcast_multiply_fusion.1), kind=kLoop, calls=%fused_computation.1 | loop fusion | flops 19922944 | bytes 2114564 | tf_op jit(solution)/shard_map/convert_element_type | solution.py:346
  7.6 17.0 %sketch.2 = (f32[3072,256]{1,0:T(8,128)S(1)}, f32[768,256]{1,0:T(8,128)S(1)}, f32[2304,256]{1,0:T(8,128)S(1)}) custom-call(s32[8,5]{1,0:T(8,128)S(1)} %pad_add_fusion.scal_ref, s32[8,4096]{1,0:T(8,128)S(1)} %broadcast_in_dim.2.ids_ref, bf16[4096,4096]{1,0:T(8,128)(2,1)} %bitcast.18, bf16[4096,256]{1,0:T(8,128)(2,1)S(1)} %multiply_convert_fusion.1.samples_ref), custom_call_target="tpu_custom_call" | custom-call | tf_op jit(solution)/shard_map/sketch/pallas_call | solution.py:162
  25.1 1.9 %collective-permute-done.refs_1_ = f32[768,256]{1,0:T(8,128)S(1)} collective-permute-done((f32[768,256]{1,0:T(8,128)S(1)}, f32[768,256]{1,0:T(8,128)S(1)}, u32[]{:S(2)}, u32[]{:S(2)}) %collective-permute-start) | collective-permute-done | bytes 786464 | tf_op jit(solution)/shard_map/ppermute | solution.py:355
  28.2 4.6 %collective-permute-start.3 = (f32[768,128]{1,0:T(8,128)S(1)}, f32[768,128]{1,0:T(8,128)S(1)}, u32[]{:S(2)}, u32[]{:S(2)}) collective-permute-start(f32[768,128]{1,0:T(8,128)S(1)} %get-tuple-element.66.refs_0_), channel_id=1, source_target_pairs={{0,1},{3,2},{4,5},{7,6},{8,9},{11,10},{12,13},{15,14},{16,17},{19,... | collective-permute-start | bytes 1179656 | tf_op jit(solution)/shard_map/ppermute | solution.py:253
  34.2 2.4 %multiply_convert_fusion.samples_ref = bf16[4096,256]{1,0:T(8,128)(2,1)S(1)} fusion(s32[]{:T(128)} %bitcast.7, s32[4096]{0:T(1024)S(1)} %broadcast_multiply_fusion, s32[256]{0:T(256)S(1)} %iota_multiply_fusion), kind=kLoop, calls=%fused_computation | loop fusion | flops 19922944 | bytes 2114564 | tf_op jit(solution)/shard_map/convert_element_type | solution.py:346
  38.1 10.0 %multiply.3 = (bf16[3072,256]{1,0:T(8,128)(2,1)S(1)}, bf16[3072,256]{1,0:T(8,128)(2,1)S(1)}) custom-call(bf16[4096,4096]{1,0:T(8,128)(2,1)} %bitcast.19, bf16[4096,256]{1,0:T(8,128)(2,1)S(1)} %multiply_convert_fusion.samples_ref), custom_call_target="tpu_custom_call" | custom-call | tf_op jit(solution)/shard_map/multiply/pallas_call | solution.py:133
  48.8 1.9 %collective-permute-done.5.refs_1_ = f32[768,128]{1,0:T(8,128)S(1)} collective-permute-done((f32[768,128]{1,0:T(8,128)S(1)}, f32[768,128]{1,0:T(8,128)S(1)}, u32[]{:S(2)}, u32[]{:S(2)}) %collective-permute-start.5) | collective-permute-done | bytes 393248 | tf_op jit(solution)/shard_map/ppermute | solution.py:253
  51.4 10.8 %sketch.3 = (f32[3072,256]{1,0:T(8,128)S(1)}, f32[768,256]{1,0:T(8,128)}, f32[2304,256]{1,0:T(8,128)}) custom-call(s32[8,5]{1,0:T(8,128)S(1)} %pad_add_fusion.scal_ref, s32[8,4096]{1,0:T(8,128)S(1)} %broadcast_in_dim.2.ids_ref, bf16[4096,4096]{1,0:T(8,128)(2,1)} %bitcast.20, bf16[4096,256]{1,0:T(8,128)(2,1)S(1)} %multiply_convert_fusion.samples_ref, ...), custom_call_target="tpu_custom_call" | custom-call | tf_op jit(solution)/shard_map/sketch/pallas_call | solution.py:162
  63.5 3.4 %collective-permute-done.2.refs_1_ = f32[768,256]{1,0:T(8,128)S(1)} collective-permute-done((f32[768,256]{1,0:T(8,128)S(1)}, f32[768,256]{1,0:T(8,128)S(1)}, u32[]{:S(2)}, u32[]{:S(2)}) %collective-permute-start.2) | collective-permute-done | bytes 786464 | tf_op jit(solution)/shard_map/ppermute | solution.py:253
  67.5 3.1 %collective-permute-start.7 = (f32[768,256]{1,0:T(8,128)}, f32[768,256]{1,0:T(8,128)}, u32[]{:S(2)}, u32[]{:S(2)}) collective-permute-start(f32[768,256]{1,0:T(8,128)} %add.225), channel_id=1, source_target_pairs={{0,1},{1,0},{2,3},{3,2},{4,5},{5,4},{6,7},{7,6},{8,9},{9,8},{10,11... | collective-permute-start | bytes 2359304 | tf_op jit(solution)/shard_map/ppermute | solution.py:253
  73.1 2.0 %add.233 = (f32[768,128]{1,0:T(8,128)}, f32[768,128]{1,0:T(8,128)S(1)}) custom-call(f32[3072,256]{1,0:T(8,128)S(1)} %get-tuple-element.82.refs_0_, f32[768,256]{1,0:T(8,128)} %collective-permute-done.11.refs_1_), custom_call_target="tpu_custom_call" | custom-call | tf_op jit(solution)/shard_map/add/pallas_call | solution.py:295
  75.1 5.6 %collective-permute-start.12 = (f32[768,128]{1,0:T(8,128)}, f32[768,128]{1,0:T(8,128)}, u32[]{:S(2)}, u32[]{:S(2)}) collective-permute-start(f32[768,128]{1,0:T(8,128)} %get-tuple-element.90.refs_0_), channel_id=1, source_target_pairs={{0,1},{3,2},{4,5},{7,6},{8,9},{11,10},{12,13},{15,14},{16,17},{19,... | collective-permute-start | bytes 1179656 | tf_op jit(solution)/shard_map/ppermute | solution.py:253
  80.7 2.1 %collective-permute-start.15 = (f32[768,128]{1,0:T(8,128)S(1)}, f32[768,128]{1,0:T(8,128)}, u32[]{:S(2)}, u32[]{:S(2)}) collective-permute-start(f32[768,128]{1,0:T(8,128)S(1)} %get-tuple-element.94.refs_0_), channel_id=1, source_target_pairs={{0,1},{3,2},{4,5},{7,6},{8,9},{11,10},{12,13},{15,14},{16,17},{19,... | collective-permute-start | bytes 1179656 | tf_op jit(solution)/shard_map/ppermute | solution.py:253
  82.8 6.0 %collective-permute-done.7.refs_1_ = f32[768,256]{1,0:T(8,128)} collective-permute-done((f32[768,256]{1,0:T(8,128)}, f32[768,256]{1,0:T(8,128)}, u32[]{:S(2)}, u32[]{:S(2)}) %collective-permute-start.7) | collective-permute-done | bytes 786464 | tf_op jit(solution)/shard_map/ppermute | solution.py:253
  91.3 2.4 %add.230.refs_0_ = f32[768,256]{1,0:T(8,128)} custom-call(f32[3072,256]{1,0:T(8,128)S(1)} %get-tuple-element.82.refs_0_, f32[2304,256]{1,0:T(8,128)} %collective-permute-done.9.refs_1_), custom_call_target="tpu_custom_call" | custom-call | tf_op jit(solution)/shard_map/add/pallas_call | solution.py:295
  97.0 5.2 %collective-permute-start.10 = (f32[768,256]{1,0:T(8,128)}, f32[768,256]{1,0:T(8,128)S(1)}, u32[]{:S(2)}, u32[]{:S(2)}) collective-permute-start(f32[768,256]{1,0:T(8,128)} %add.230.refs_0_), channel_id=1, source_target_pairs={{0,1},{3,2},{4,5},{7,6},{8,9},{11,10},{12,13},{15,14},{16,17},{19,... | collective-permute-start | bytes 2359304 | tf_op jit(solution)/shard_map/ppermute | solution.py:253
  108.8 5.8 %collective-permute-start.17 = (f32[128,256]{1,0:T(8,128)S(1)}, f32[128,256]{1,0:T(8,128)S(1)}, u32[]{:S(2)}, u32[]{:S(2)}) collective-permute-start(f32[128,256]{1,0:T(8,128)S(1)} %dynamic-slice_add_fusion.1), channel_id=1, source_target_pairs={{0,1},{3,2},{4,5},{7,6},{8,9},{11,10},{12,13},{15,14},{16,17},{19,... | collective-permute-start | bytes 393224 | tf_op jit(solution)/shard_map/ppermute | solution.py:253
  114.6 9.7 %collective-permute-done.17 = f32[128,256]{1,0:T(8,128)S(1)} collective-permute-done((f32[128,256]{1,0:T(8,128)S(1)}, f32[128,256]{1,0:T(8,128)S(1)}, u32[]{:S(2)}, u32[]{:S(2)}) %collective-permute-start.17) | collective-permute-done | bytes 131104 | tf_op jit(solution)/shard_map/ppermute | solution.py:253
  124.5 2.9 %collective-permute-start.18 = (f32[768,256]{1,0:T(8,128)S(1)}, f32[768,256]{1,0:T(8,128)S(1)}, u32[]{:S(2)}, u32[]{:S(2)}) collective-permute-start(f32[768,256]{1,0:T(8,128)S(1)} %add.236), channel_id=1, source_target_pairs={{0,1},{1,0},{2,3},{3,2},{4,5},{5,4},{6,7},{7,6},{8,9},{9,8},{10,11... | collective-permute-start | bytes 2359304 | tf_op jit(solution)/shard_map/ppermute | solution.py:253
  130.2 14.2 %collective-permute-done.18.refs_1_ = f32[768,256]{1,0:T(8,128)S(1)} collective-permute-done((f32[768,256]{1,0:T(8,128)S(1)}, f32[768,256]{1,0:T(8,128)S(1)}, u32[]{:S(2)}, u32[]{:S(2)}) %collective-permute-start.18) | collective-permute-done | bytes 786464 | tf_op jit(solution)/shard_map/ppermute | solution.py:253
  147.5 6.2 %collective-permute-start.21 = (f32[128,256]{1,0:T(8,128)S(1)}, f32[128,256]{1,0:T(8,128)S(1)}, u32[]{:S(2)}, u32[]{:S(2)}) collective-permute-start(f32[128,256]{1,0:T(8,128)S(1)} %dynamic-slice_add_fusion), channel_id=1, source_target_pairs={{0,1},{1,0},{2,3},{3,2},{4,5},{5,4},{6,7},{7,6},{8,9},{9,8},{10,11... | collective-permute-start | bytes 393224 | tf_op jit(solution)/shard_map/ppermute | solution.py:253
  153.7 4.2 %collective-permute-done.23 = f32[128,256]{1,0:T(8,128)S(1)} collective-permute-done((f32[128,256]{1,0:T(8,128)S(1)}, f32[128,256]{1,0:T(8,128)S(1)}, u32[]{:S(2)}, u32[]{:S(2)}) %collective-permute-start.23) | collective-permute-done | bytes 131104 | tf_op jit(solution)/shard_map/ppermute | solution.py:253
  158.0 2.6 %collective-permute-done.21 = f32[128,256]{1,0:T(8,128)S(1)} collective-permute-done((f32[128,256]{1,0:T(8,128)S(1)}, f32[128,256]{1,0:T(8,128)S(1)}, u32[]{:S(2)}, u32[]{:S(2)}) %collective-permute-start.21) | collective-permute-done | bytes 131104 | tf_op jit(solution)/shard_map/ppermute | solution.py:253
  162.0 8.9 %inverse_factor.1 = f32[256,256]{1,0:T(8,128)S(1)} custom-call(f32[256,256]{1,0:T(8,128)S(1)} %maximum_multiply_fusion.gram_ref), custom_call_target="tpu_custom_call" | custom-call | tf_op jit(solution)/shard_map/inverse_factor/pallas_call | solution.py:235
  (108 shorter events, 37.7 us)
Async XLA Ops:
  24.6 2.4 %collective-permute-start = (f32[768,256]{1,0:T(8,128)S(1)}, f32[768,256]{1,0:T(8,128)S(1)}, u32[]{:S(2)}, u32[]{:S(2)}) collective-permute-start(f32[768,256]{1,0:T(8,128)S(1)} %get-tuple-element.55), channel_id=1, source_target_pairs={{0,16},{16,0},{1,17},{17,1},{2,18},{18,2},{3,19},{19,3},{4,20},{20... | collective-permute-start | bytes 2359304 | tf_op jit(solution)/shard_map/ppermute | solution.py:355
  27.2 9.5 %collective-permute-start.1 = (f32[2304,256]{1,0:T(8,128)S(1)}, f32[2304,256]{1,0:T(8,128)S(1)}, u32[]{:S(2)}, u32[]{:S(2)}) collective-permute-start(f32[2304,256]{1,0:T(8,128)S(1)} %get-tuple-element.60), channel_id=1, source_target_pairs={{0,16},{16,0},{1,17},{17,1},{2,18},{18,2},{3,19},{19,3},{4,20},{20... | collective-permute-start | bytes 7077896 | tf_op jit(solution)/shard_map/ppermute | solution.py:355
  28.2 19.8 %collective-permute-start.3 = (f32[768,128]{1,0:T(8,128)S(1)}, f32[768,128]{1,0:T(8,128)S(1)}, u32[]{:S(2)}, u32[]{:S(2)}) collective-permute-start(f32[768,128]{1,0:T(8,128)S(1)} %get-tuple-element.66.refs_0_), channel_id=1, source_target_pairs={{0,1},{3,2},{4,5},{7,6},{8,9},{11,10},{12,13},{15,14},{16,17},{19,... | collective-permute-start | bytes 1179656 | tf_op jit(solution)/shard_map/ppermute | solution.py:253
  32.8 17.8 %collective-permute-start.5 = (f32[768,128]{1,0:T(8,128)S(1)}, f32[768,128]{1,0:T(8,128)S(1)}, u32[]{:S(2)}, u32[]{:S(2)}) collective-permute-start(f32[768,128]{1,0:T(8,128)S(1)} %get-tuple-element.71.refs_0_), channel_id=1, source_target_pairs={{0,1},{3,2},{4,5},{7,6},{8,9},{11,10},{12,13},{15,14},{16,17},{19,... | collective-permute-start | bytes 1179656 | tf_op jit(solution)/shard_map/ppermute | solution.py:253
  36.7 30.2 %collective-permute-start.2 = (f32[768,256]{1,0:T(8,128)S(1)}, f32[768,256]{1,0:T(8,128)S(1)}, u32[]{:S(2)}, u32[]{:S(2)}) collective-permute-start(f32[768,256]{1,0:T(8,128)S(1)} %add.221.refs_0_), channel_id=1, source_target_pairs={{0,1},{3,2},{4,5},{7,6},{8,9},{11,10},{12,13},{15,14},{16,17},{19,... | collective-permute-start | bytes 2359304 | tf_op jit(solution)/shard_map/ppermute | solution.py:253
  48.1 14.2 %collective-permute-start.4 = (f32[768,128]{1,0:T(8,128)S(1)}, f32[768,128]{1,0:T(8,128)S(1)}, u32[]{:S(2)}, u32[]{:S(2)}) collective-permute-start(f32[768,128]{1,0:T(8,128)S(1)} %add.223), channel_id=1, source_target_pairs={{1,2},{2,1},{5,6},{6,5},{9,10},{10,9},{13,14},{14,13},{17,18},{18,... | collective-permute-start | bytes 1179656 | tf_op jit(solution)/shard_map/ppermute | solution.py:253
  50.7 11.7 %collective-permute-start.6 = (f32[768,128]{1,0:T(8,128)S(1)}, f32[768,128]{1,0:T(8,128)S(1)}, u32[]{:S(2)}, u32[]{:S(2)}) collective-permute-start(f32[768,128]{1,0:T(8,128)S(1)} %add.224), channel_id=1, source_target_pairs={{1,2},{2,1},{5,6},{6,5},{9,10},{10,9},{13,14},{14,13},{17,18},{18,... | collective-permute-start | bytes 1179656 | tf_op jit(solution)/shard_map/ppermute | solution.py:253
  67.0 24.4 %collective-permute-start.9 = (f32[2304,256]{1,0:T(8,128)}, f32[2304,256]{1,0:T(8,128)}, u32[]{:S(2)}, u32[]{:S(2)}) collective-permute-start(f32[2304,256]{1,0:T(8,128)} %get-tuple-element.83), channel_id=1, source_target_pairs={{0,16},{16,0},{1,17},{17,1},{2,18},{18,2},{3,19},{19,3},{4,20},{20... | collective-permute-start | bytes 7077896 | tf_op jit(solution)/shard_map/ppermute | solution.py:355
  67.0 6.2 %collective-permute-start.11 = (f32[768,256]{1,0:T(8,128)}, f32[768,256]{1,0:T(8,128)}, u32[]{:S(2)}, u32[]{:S(2)}) collective-permute-start(f32[768,256]{1,0:T(8,128)} %get-tuple-element.88), channel_id=1, source_target_pairs={{0,16},{16,0},{1,17},{17,1},{2,18},{18,2},{3,19},{19,3},{4,20},{20... | collective-permute-start | bytes 2359304 | tf_op jit(solution)/shard_map/ppermute | solution.py:355
  67.5 21.4 %collective-permute-start.7 = (f32[768,256]{1,0:T(8,128)}, f32[768,256]{1,0:T(8,128)}, u32[]{:S(2)}, u32[]{:S(2)}) collective-permute-start(f32[768,256]{1,0:T(8,128)} %add.225), channel_id=1, source_target_pairs={{0,1},{1,0},{2,3},{3,2},{4,5},{5,4},{6,7},{7,6},{8,9},{9,8},{10,11... | collective-permute-start | bytes 2359304 | tf_op jit(solution)/shard_map/ppermute | solution.py:253
  71.6 18.5 %collective-permute-start.8 = (f32[768,256]{1,0:T(8,128)}, f32[768,256]{1,0:T(8,128)}, u32[]{:S(2)}, u32[]{:S(2)}) collective-permute-start(f32[768,256]{1,0:T(8,128)} %add.228), channel_id=1, source_target_pairs={{1,2},{2,1},{5,6},{6,5},{9,10},{10,9},{13,14},{14,13},{17,18},{18,... | collective-permute-start | bytes 2359304 | tf_op jit(solution)/shard_map/ppermute | solution.py:253
  75.1 30.1 %collective-permute-start.12 = (f32[768,128]{1,0:T(8,128)}, f32[768,128]{1,0:T(8,128)}, u32[]{:S(2)}, u32[]{:S(2)}) collective-permute-start(f32[768,128]{1,0:T(8,128)} %get-tuple-element.90.refs_0_), channel_id=1, source_target_pairs={{0,1},{3,2},{4,5},{7,6},{8,9},{11,10},{12,13},{15,14},{16,17},{19,... | collective-permute-start | bytes 1179656 | tf_op jit(solution)/shard_map/ppermute | solution.py:253
  80.7 26.3 %collective-permute-start.15 = (f32[768,128]{1,0:T(8,128)S(1)}, f32[768,128]{1,0:T(8,128)}, u32[]{:S(2)}, u32[]{:S(2)}) collective-permute-start(f32[768,128]{1,0:T(8,128)S(1)} %get-tuple-element.94.refs_0_), channel_id=1, source_target_pairs={{0,1},{3,2},{4,5},{7,6},{8,9},{11,10},{12,13},{15,14},{16,17},{19,... | collective-permute-start | bytes 1179656 | tf_op jit(solution)/shard_map/ppermute | solution.py:253
  97.0 27.4 %collective-permute-start.10 = (f32[768,256]{1,0:T(8,128)}, f32[768,256]{1,0:T(8,128)S(1)}, u32[]{:S(2)}, u32[]{:S(2)}) collective-permute-start(f32[768,256]{1,0:T(8,128)} %add.230.refs_0_), channel_id=1, source_target_pairs={{0,1},{3,2},{4,5},{7,6},{8,9},{11,10},{12,13},{15,14},{16,17},{19,... | collective-permute-start | bytes 2359304 | tf_op jit(solution)/shard_map/ppermute | solution.py:253
  106.4 18.0 %collective-permute-start.14 = (f32[768,128]{1,0:T(8,128)S(1)}, f32[768,128]{1,0:T(8,128)S(1)}, u32[]{:S(2)}, u32[]{:S(2)}) collective-permute-start(f32[768,128]{1,0:T(8,128)S(1)} %add.234), channel_id=1, source_target_pairs={{1,2},{2,1},{5,6},{6,5},{9,10},{10,9},{13,14},{14,13},{17,18},{18,... | collective-permute-start | bytes 1179656 | tf_op jit(solution)/shard_map/ppermute | solution.py:253
  108.1 16.2 %collective-permute-start.16 = (f32[768,128]{1,0:T(8,128)S(1)}, f32[768,128]{1,0:T(8,128)S(1)}, u32[]{:S(2)}, u32[]{:S(2)}) collective-permute-start(f32[768,128]{1,0:T(8,128)S(1)} %add.235), channel_id=1, source_target_pairs={{1,2},{2,1},{5,6},{6,5},{9,10},{10,9},{13,14},{14,13},{17,18},{18,... | collective-permute-start | bytes 1179656 | tf_op jit(solution)/shard_map/ppermute | solution.py:253
  108.8 15.5 %collective-permute-start.17 = (f32[128,256]{1,0:T(8,128)S(1)}, f32[128,256]{1,0:T(8,128)S(1)}, u32[]{:S(2)}, u32[]{:S(2)}) collective-permute-start(f32[128,256]{1,0:T(8,128)S(1)} %dynamic-slice_add_fusion.1), channel_id=1, source_target_pairs={{0,1},{3,2},{4,5},{7,6},{8,9},{11,10},{12,13},{15,14},{16,17},{19,... | collective-permute-start | bytes 393224 | tf_op jit(solution)/shard_map/ppermute | solution.py:253
  124.5 19.9 %collective-permute-start.18 = (f32[768,256]{1,0:T(8,128)S(1)}, f32[768,256]{1,0:T(8,128)S(1)}, u32[]{:S(2)}, u32[]{:S(2)}) collective-permute-start(f32[768,256]{1,0:T(8,128)S(1)} %add.236), channel_id=1, source_target_pairs={{0,1},{1,0},{2,3},{3,2},{4,5},{5,4},{6,7},{7,6},{8,9},{9,8},{10,11... | collective-permute-start | bytes 2359304 | tf_op jit(solution)/shard_map/ppermute | solution.py:253
  128.6 15.9 %collective-permute-start.19 = (f32[768,256]{1,0:T(8,128)S(1)}, f32[768,256]{1,0:T(8,128)S(1)}, u32[]{:S(2)}, u32[]{:S(2)}) collective-permute-start(f32[768,256]{1,0:T(8,128)S(1)} %add.238), channel_id=1, source_target_pairs={{1,2},{2,1},{5,6},{6,5},{9,10},{10,9},{13,14},{14,13},{17,18},{18,... | collective-permute-start | bytes 2359304 | tf_op jit(solution)/shard_map/ppermute | solution.py:253
  129.5 16.6 %collective-permute-start.22 = (f32[128,256]{1,0:T(8,128)S(1)}, f32[128,256]{1,0:T(8,128)S(1)}, u32[]{:S(2)}, u32[]{:S(2)}) collective-permute-start(f32[128,256]{1,0:T(8,128)S(1)} %add.190), channel_id=1, source_target_pairs={{1,2},{2,1},{5,6},{6,5},{9,10},{10,9},{13,14},{14,13},{17,18},{18,... | collective-permute-start | bytes 393224 | tf_op jit(solution)/shard_map/ppermute | solution.py:253
  146.0 1.4 collective-permute-start.20
  146.2 11.8 %collective-permute-start.23 = (f32[128,256]{1,0:T(8,128)S(1)}, f32[128,256]{1,0:T(8,128)S(1)}, u32[]{:S(2)}, u32[]{:S(2)}) collective-permute-start(f32[128,256]{1,0:T(8,128)S(1)} %add.193), channel_id=1, source_target_pairs={{1,0},{2,3},{5,4},{6,7},{9,8},{10,11},{13,12},{14,15},{17,16},{18,... | collective-permute-start | bytes 393224 | tf_op jit(solution)/shard_map/ppermute | solution.py:253
  147.5 13.0 %collective-permute-start.21 = (f32[128,256]{1,0:T(8,128)S(1)}, f32[128,256]{1,0:T(8,128)S(1)}, u32[]{:S(2)}, u32[]{:S(2)}) collective-permute-start(f32[128,256]{1,0:T(8,128)S(1)} %dynamic-slice_add_fusion), channel_id=1, source_target_pairs={{0,1},{1,0},{2,3},{3,2},{4,5},{5,4},{6,7},{7,6},{8,9},{9,8},{10,11... | collective-permute-start | bytes 393224 | tf_op jit(solution)/shard_map/ppermute | solution.py:253
  160.7 12.0 %collective-permute-start.24 = (f32[128,256]{1,0:T(8,128)S(1)}, f32[128,256]{1,0:T(8,128)S(1)}, u32[]{:S(2)}, u32[]{:S(2)}) collective-permute-start(f32[128,256]{1,0:T(8,128)S(1)} %add.192), channel_id=1, source_target_pairs={{0,2},{2,0},{1,3},{3,1},{4,6},{6,4},{5,7},{7,5},{8,10},{10,8},{9,1... | collective-permute-start | bytes 393224 | tf_op jit(solution)/shard_map/ppermute | solution.py:253
  (12 other events, 140.0 us)
